TPU v7x, 32 devices: a whole 2x2x4 slice. The times are simulated.
32 devices in a mesh: tile: 8 (over y, x, core), slab: 4 (over z).
Axes of the slice: x: 2, y: 2, z: 4, core: 2. Of those that a mesh axis runs over, the one named last changes fastest.
Arguments:
- stored: float32 [32, 8, 256, 1024], P('tile', 'slab'), may hold values from -6 to 6
- offsets: int32 [2, 2, 32], P(None, None, ('tile', 'slab')), may hold values from 0 to 128
Outputs:
- surface: float32 [2, 32, 128, 1024], P(None, ('tile', 'slab'))
- peak: float32 [2, 32], P(None, ('tile', 'slab'))
All inputs are finite; a program needn't handle non-finite values.
Results may differ from a plain program's by a relative error of at most 0.0003.
Values sent between devices are 32-bit elements; how exact they have to be, the bound alone decides.
A program may use at most 192 MiB of HBM per device.

v0:
```python
import functools
import math

import jax
import jax.numpy as jnp
import numpy as np
from jax import lax
from jax.experimental import pallas as pl
from jax.experimental.pallas import tpu as pltpu
from jax.sharding import PartitionSpec as P

A = 128
GC = 7
ROUNDS = 2
FLOOR = 0.25
LANES = 128
F32 = jnp.float32
BF16 = jnp.bfloat16


def halves(table):
    high = table.astype(np.float32).astype(BF16)
    low = (table - high.astype(np.float64)).astype(np.float32).astype(BF16)
    return jnp.asarray(high), jnp.asarray(low)


def phases(rows, cols, total):
    angle = (np.outer(rows, cols) % total) * (2.0 * math.pi / total)
    return np.cos(angle), np.sin(angle)


def make_tables(depth, across, along):
    quarter = along // 4
    half = quarter // 2
    scale = 1.0 / math.sqrt(depth * across * along)
    at = np.arange(quarter)
    cos0, sin0 = phases(at, 4 * np.arange(half), along)
    sin0 = -sin0
    sin0[:, 0] = np.where(at % 2 == 0, 1.0, -1.0)
    first = np.concatenate((cos0, sin0), axis=1) * scale
    cos2, sin2 = phases(at, 4 * np.arange(half) + 2, along)
    second = np.concatenate((cos2, -sin2), axis=1) * scale
    cos1, sin1 = phases(at, 4 * np.arange(quarter) + 1, along)
    third = np.block([[cos1, -sin1], [-sin1, -cos1]]) * scale
    weight = np.full((2 * half, 1), 2.0)
    weight[0] = weight[half] = 1.0
    cos_a, sin_a = phases(np.arange(across), np.arange(across), across)
    rows = np.block([[cos_a, sin_a], [-sin_a, cos_a]])
    cos_z, sin_z = phases(np.arange(depth), np.arange(depth), depth)
    planes = np.zeros((2 * LANES, 2 * LANES))
    planes[:depth, :depth] = cos_z
    planes[:depth, LANES : LANES + depth] = -sin_z
    planes[LANES : LANES + depth, :depth] = sin_z
    planes[LANES : LANES + depth, LANES : LANES + depth] = cos_z
    forth = [first, second, third, rows, planes]
    back = [first.T * weight, second.T * 2.0, third.T * 2.0, rows.T, planes.T]
    flat = lambda group: [part for table in group for part in halves(table)]
    return flat(forth), flat(back)


def split(x):
    high = x.astype(BF16)
    return high, (x - high.astype(F32)).astype(BF16)


def dot(a, b):
    return jnp.dot(a, b, preferred_element_type=F32)


def by_right(x, high, low):
    xh, xl = split(x)
    return dot(xh, high[...]) + (dot(xl, high[...]) + dot(xh, low[...]))


def by_left(high, low, x):
    xh, xl = split(x)
    return dot(high[...], xh) + (dot(high[...], xl) + dot(low[...], xh))


def fft(points, sign):
    n = len(points)
    if n == 1:
        return points
    even = fft(points[0::2], sign)
    odd = fft(points[1::2], sign)
    out = [None] * n
    for k in range(n // 2):
        re, im = odd[k]
        if k == 0:
            pass
        elif 4 * k == n:
            re, im = (-im, re) if sign > 0 else (im, -re)
        elif 8 * k == n:
            r = math.sqrt(0.5)
            re, im = ((re - im) * r, (im + re) * r) if sign > 0 else ((re + im) * r, (im - re) * r)
        elif 8 * k == 3 * n:
            r = math.sqrt(0.5)
            re, im = ((-re - im) * r, (re - im) * r) if sign > 0 else ((im - re) * r, (-im - re) * r)
        else:
            c = math.cos(2.0 * math.pi * k / n)
            s = sign * math.sin(2.0 * math.pi * k / n)
            re, im = re * c - im * s, im * c + re * s
        out[k] = (even[k][0] + re, even[k][1] + im)
        out[k + n // 2] = (even[k][0] - re, even[k][1] - im)
    return out


def whiten(own, partner, keep):
    re = own[0] * partner[0] + own[1] * partner[1]
    im = own[1] * partner[0] - own[0] * partner[1]
    gain = lax.rsqrt(jnp.maximum(re * re + im * im, FLOOR * FLOOR)) * keep
    return re * gain, im * gain


def lane_is(shape, lane):
    return lax.broadcasted_iota(jnp.int32, shape, 1) == lane


def spectrum(strip, tabs, spec, edge, column):
    f0h, f0l, f2h, f2l, f1h, f1l, rh, rl, zh, zl = tabs
    depth, across, along = strip.shape
    q = along // 4
    h = q // 2
    column[...] = jnp.zeros_like(column)

    def step(i, carry):
        x = strip[pl.ds(2 * i, 2)].reshape(2 * across, along)
        x0, x1, x2, x3 = (x[:, n * q : (n + 1) * q] for n in range(4))
        s02, s13 = x0 + x2, x1 + x3
        out0 = by_right(s02 + s13, f0h, f0l)
        out2 = by_right(s02 - s13, f2h, f2l)
        out1 = by_right(jnp.concatenate((x0 - x2, x1 - x3), axis=1), f1h, f1l)
        imag0 = out0[:, h:]
        first = lane_is(imag0.shape, 0)
        real = jnp.concatenate((out0[:, :h], out2[:, :h], out1[:, :q]), axis=1)
        imag = jnp.concatenate((jnp.where(first, 0.0, imag0), out2[:, h:], out1[:, q:]), axis=1)
        for n in range(2):
            rows = slice(n * across, (n + 1) * across)
            at = 2 * i + n
            packed = jnp.concatenate((real[rows], imag[rows]), axis=0)
            spec[at] = by_left(rh, rl, packed)
            middle = jnp.broadcast_to(imag0[rows, 0:1], column.shape)
            column[...] = jnp.where(lane_is(column.shape, at), middle, column[...])
        return carry

    lax.fori_loop(0, depth // 2, step, 0)
    turned = by_left(rh.at[:, :across], rl.at[:, :across], column[...])
    turned = jnp.concatenate((turned[:across], turned[across:]), axis=1)
    edge[...] = by_right(turned, zh, zl)


def spectrum_kernel(strip, *refs):
    tabs, (spec, edge, column) = refs[:10], refs[10:]
    spectrum(strip, tabs, spec, edge, column)


def pair_kernel(keep_ref, strip, own, own_edge, *refs):
    forth, back = refs[:10], refs[10:20]
    surface, peak, spec, edge, column = refs[20:]
    b0h, b0l, b2h, b2l, b1h, b1l, rh, rl, zh, zl = back
    depth, across, along = strip.shape
    q = along // 4
    h = q // 2
    spectrum(strip, forth, spec, edge, column)
    keep = keep_ref[0]

    def meet(i, carry):
        re_rows = pl.ds(pl.multiple_of(8 * i, 8), 8)
        im_rows = pl.ds(pl.multiple_of(across + 8 * i, 8), 8)
        for lane in range(0, along // 2, LANES):
            lanes = slice(lane, lane + LANES)
            mine = fft([(own[z, re_rows, lanes], own[z, im_rows, lanes]) for z in range(depth)], -1)
            other = fft([(spec[z, re_rows, lanes], spec[z, im_rows, lanes]) for z in range(depth)], -1)
            white = [whiten(a, b, keep) for a, b in zip(mine, other)]
            for z, (re, im) in enumerate(fft(white, 1)):
                spec[z, re_rows, lanes] = re
                spec[z, im_rows, lanes] = im
        return carry

    lax.fori_loop(0, across // 8, meet, 0)
    re, im = whiten(
        (own_edge[:, :LANES], own_edge[:, LANES:]), (edge[:, :LANES], edge[:, LANES:]), keep
    )
    back_z = by_right(jnp.concatenate((re, im), axis=1), zh, zl)
    back_z = jnp.concatenate((back_z[:, :LANES], back_z[:, LANES:]), axis=0)
    column[...] = by_left(rh.at[:across], rl.at[:across], back_z)

    surface[...] = jnp.full_like(surface, -jnp.inf)

    def step(i, carry):
        parts = []
        for n in range(2):
            at = 2 * i + n
            plane = by_left(rh, rl, spec[at])
            middle = jnp.sum(
                jnp.where(lane_is(column.shape, at), column[...], 0.0), axis=1, keepdims=True
            )
            imag0 = plane[across:, :h]
            imag0 = jnp.where(lane_is(imag0.shape, 0), middle, imag0)
            parts.append((plane[:across], imag0, plane[across:, h:]))
        real = jnp.concatenate([p[0] for p in parts], axis=0)
        imag0 = jnp.concatenate([p[1] for p in parts], axis=0)
        imag = jnp.concatenate([p[2] for p in parts], axis=0)
        z0 = by_right(jnp.concatenate((real[:, :h], imag0), axis=1), b0h, b0l)
        z2 = by_right(jnp.concatenate((real[:, h:q], imag[:, :h]), axis=1), b2h, b2l)
        z1 = by_right(jnp.concatenate((real[:, q:], imag[:, h:]), axis=1), b1h, b1l)
        plus, minus = z0 + z2, z0 - z2
        a, b = z1[:, :q], z1[:, q:]
        for n, part in enumerate((plus + a, minus + b, plus - a, minus - b)):
            lanes = slice(n * q, (n + 1) * q)
            best = jnp.maximum(part[:across], part[across:])
            surface[:, lanes] = jnp.maximum(surface[:, lanes], best)
        return carry

    lax.fori_loop(0, depth // 2, step, 0)
    peak[...] = jnp.broadcast_to(jnp.max(surface[...]), peak.shape)


VMEM = pl.BlockSpec(memory_space=pltpu.VMEM)
SMEM = pl.BlockSpec(memory_space=pltpu.SMEM)
PARAMS = pltpu.CompilerParams(vmem_limit_bytes=56 * 1024 * 1024)


def spectrum_of(strip, forth):
    depth, across, along = strip.shape
    return pl.pallas_call(
        spectrum_kernel,
        out_shape=(
            jax.ShapeDtypeStruct((depth, 2 * across, along // 2), F32),
            jax.ShapeDtypeStruct((across, 2 * LANES), F32),
        ),
        in_specs=[VMEM] * (1 + len(forth)),
        out_specs=(VMEM, VMEM),
        scratch_shapes=[pltpu.VMEM((across, LANES), F32)],
        compiler_params=PARAMS,
        cost_estimate=pl.CostEstimate(flops=8 * 10**9, bytes_accessed=2 * strip.size * 4, transcendentals=0),
    )(strip, *forth)


def pair_of(keep, strip, own, own_edge, forth, back):
    depth, across, along = strip.shape
    return pl.pallas_call(
        pair_kernel,
        out_shape=(
            jax.ShapeDtypeStruct((across, along), F32),
            jax.ShapeDtypeStruct((8, LANES), F32),
        ),
        in_specs=[SMEM] + [VMEM] * (3 + len(forth) + len(back)),
        out_specs=(VMEM, VMEM),
        scratch_shapes=[
            pltpu.VMEM((depth, 2 * across, along // 2), F32),
            pltpu.VMEM((across, 2 * LANES), F32),
            pltpu.VMEM((across, LANES), F32),
        ],
        compiler_params=PARAMS,
        cost_estimate=pl.CostEstimate(flops=16 * 10**9, bytes_accessed=2 * strip.size * 4, transcendentals=0),
    )(keep, strip, own, own_edge, *forth, *back)


def from_behind(x, axis, by):
    size = lax.axis_size(axis)
    pairs = [(i, i + by) for i in range(size) if 0 <= i + by < size]
    return lax.ppermute(x, axis, pairs)


def on_device(stored, offsets):
    axes = ("tile", "slab")
    owned = lax.all_to_all(stored, "slab", split_axis=0, concat_axis=1, tiled=True)[0]
    depth, _, along = owned.shape
    forth, back = make_tables(depth, A, along)
    count = lax.axis_size(axes)
    place = lax.axis_index(axes)
    cut = lambda rnd, which: lax.dynamic_slice_in_dim(owned, offsets[rnd, which, 0], A, 1)
    arrived = [from_behind(cut(rnd, 1), axes, -(1 if rnd == 0 else GC)) for rnd in range(ROUNDS)]
    own = [spectrum_of(cut(rnd, 0), forth) for rnd in range(ROUNDS)]
    surfaces, peaks = [], []
    for rnd in range(ROUNDS):
        if rnd == 0:
            valid = jnp.logical_and(place % GC != GC - 1, place + 1 < count)
        else:
            valid = place + GC < count
        surface, peak = pair_of(
            valid.astype(F32).reshape(1), arrived[rnd], *own[rnd], forth, back
        )
        surfaces.append(surface)
        peaks.append(peak[0, 0])
    return jnp.stack(surfaces)[:, None], jnp.stack(peaks)[:, None]


def solution(mesh):
    return jax.shard_map(
        on_device,
        mesh=mesh,
        in_specs=(P("tile", "slab", None, None), P(None, None, ("tile", "slab"))),
        out_specs=(P(None, ("tile", "slab"), None, None), P(None, ("tile", "slab"))),
        check_vma=False,
    )
```

profile of v0, /device:TPU:2, one launch (start us, length us, event | category | flops | bytes accessed | tf_op | source)
XLA Modules:
  0.0 432.4 jit_solution(13017036656395577788)
XLA Ops:
  0.6 0.0 copy-start.1
  0.6 5.7 %all-to-all-start = ((f32[4,2,256,1024]{3,2,1,0:T(8,128)}), f32[4,2,256,1024]{3,2,1,0:T(8,128)}, u32[]{:S(2)}, u32[]{:S(2)}) async-start(f32[4,2,256,1024]{3,2,1,0:T(8,128)} %param.22), calls=%async_computation | async-start | bytes 16777216 | tf_op jit(solution)/shard_map/all_to_all | solution.py:268
  6.3 0.0 copy-done.1
  6.3 0.7 fusion
  14.6 175.0 %all-to-all-done = f32[4,2,256,1024]{3,2,1,0:T(8,128)} async-done(((f32[4,2,256,1024]{3,2,1,0:T(8,128)}), f32[4,2,256,1024]{3,2,1,0:T(8,128)}, u32[]{:S(2)}, u32[]{:S(2)}) %all-to-all-start) | async-done | bytes 8388640 | tf_op jit(solution)/shard_map/all_to_all | solution.py:268
  189.7 12.5 %constant_dynamic-slice_fusion.2 = (f32[8,128,1024]{2,1,0:T(8,128)}, f32[8,128,1024]{2,1,0:T(8,128)}, f32[8,128,1024]{2,1,0:T(8,128)}, f32[8,128,1024]{2,1,0:T(8,128)}) fusion(f32[8,256,1024]{2,1,0:T(8,128)} %bitcast.1, s32[]{:T(128)S(6)} %select_n.21, s32[]{:T(128)S(6)} %select_n.23, s32[]{:T(128)S(6)} %select_n.22, s32[]{:T(128)S(6)} %select_n.20), kind=kLoop, calls=%fused_computation.3 | loop fusion | bytes 33554448 | tf_op jit(solution)/shard_map/dynamic_slice | solution.py:273
  202.1 2.1 collective-permute-start
  204.2 3.7 collective-permute-start.1
  208.0 10.1 %shard_map.221 = (f32[8,256,512]{2,1,0:T(8,128)}, f32[128,256]{1,0:T(8,128)}) custom-call(f32[8,128,1024]{2,1,0:T(8,128)} %get-tuple-element.20.strip, bf16[256,256]{1,0:T(8,128)(2,1)} %constant.70.clone.refs_0_, bf16[256,256]{1,0:T(8,128)(2,1)} %constant.71.clone.refs_1_, bf16[256,256]{1,0:T(8,128)(2,1)} %constant.72.clone.refs_2_, ...), custom_call_target="tpu_custom_call" | custom-call | flops 8000000000 | bytes 8388608 | tf_op jit(solution)/shard_map/pallas_call | solution.py:226
  218.0 10.0 %shard_map.223 = (f32[8,256,512]{2,1,0:T(8,128)}, f32[128,256]{1,0:T(8,128)}) custom-call(f32[8,128,1024]{2,1,0:T(8,128)} %get-tuple-element.21.strip, bf16[256,256]{1,0:T(8,128)(2,1)} %constant.70.clone.refs_0_, bf16[256,256]{1,0:T(8,128)(2,1)} %constant.71.clone.refs_1_, bf16[256,256]{1,0:T(8,128)(2,1)} %constant.72.clone.refs_2_, ...), custom_call_target="tpu_custom_call" | custom-call | flops 8000000000 | bytes 8388608 | tf_op jit(solution)/shard_map/pallas_call | solution.py:226
  228.1 157.6 %collective-permute-done.strip = f32[8,128,1024]{2,1,0:T(8,128)} collective-permute-done((f32[8,128,1024]{2,1,0:T(8,128)}, f32[8,128,1024]{2,1,0:T(8,128)}, u32[]{:S(2)}, u32[]{:S(2)}) %collective-permute-start) | collective-permute-done | bytes 4194336 | tf_op jit(solution)/shard_map/ppermute | solution.py:263
  385.7 20.1 %shard_map.222 = (f32[128,1024]{1,0:T(8,128)}, f32[8,128]{1,0:T(8,128)}) custom-call(f32[1]{0:T(128)} %bitcast.keep_ref, f32[8,128,1024]{2,1,0:T(8,128)} %collective-permute-done.strip, f32[8,256,512]{2,1,0:T(8,128)} %get-tuple-element.10.own, f32[128,256]{1,0:T(8,128)} %get-tuple-element.11.own_edge, bf16[256,256]{1,0:T(8,128)(2,1)} %constant.70.clone.refs_0_, ...), custom_call_target="tpu_custom_call" | custom-call | flops 16000000000 | bytes 8388608 | tf_op jit(solution)/shard_map/pallas_call | solution.py:242
  405.8 1.3 slice.22
  407.0 0.0 collective-permute-done.1.strip
  407.0 0.0 copy-start
  407.0 20.1 %shard_map.224 = (f32[128,1024]{1,0:T(8,128)}, f32[8,128]{1,0:T(8,128)}) custom-call(f32[1]{0:T(128)} %bitcast.5.keep_ref, f32[8,128,1024]{2,1,0:T(8,128)} %collective-permute-done.1.strip, f32[8,256,512]{2,1,0:T(8,128)} %get-tuple-element.13.own, f32[128,256]{1,0:T(8,128)} %get-tuple-element.14.own_edge, bf16[256,256]{1,0:T(8,128)(2,1)} %constant.70.clone.refs_0_, ...), custom_call_target="tpu_custom_call" | custom-call | flops 16000000000 | bytes 8388608 | tf_op jit(solution)/shard_map/pallas_call | solution.py:242
  427.2 1.2 slice.23
  428.4 1.9 maximum_bitcast_fusion.1
  430.3 0.0 copy-done
  430.3 2.1 maximum_bitcast_fusion
Async XLA Ops:
  0.6 5.7 %copy-start.1 = (s32[2,2,1]{1,2,0:T(1,128)S(1)}, s32[2,2,1]{1,2,0:T(1,128)}, u32[]{:S(2)}) copy-start(s32[2,2,1]{1,2,0:T(1,128)} %param.23) | copy-start | bytes 52
  0.6 189.0 %all-to-all-start = ((f32[4,2,256,1024]{3,2,1,0:T(8,128)}), f32[4,2,256,1024]{3,2,1,0:T(8,128)}, u32[]{:S(2)}, u32[]{:S(2)}) async-start(f32[4,2,256,1024]{3,2,1,0:T(8,128)} %param.22), calls=%async_computation | async-start | bytes 16777216 | tf_op jit(solution)/shard_map/all_to_all | solution.py:268
  202.1 183.6 %collective-permute-start = (f32[8,128,1024]{2,1,0:T(8,128)}, f32[8,128,1024]{2,1,0:T(8,128)}, u32[]{:S(2)}, u32[]{:S(2)}) collective-permute-start(f32[8,128,1024]{2,1,0:T(8,128)} %get-tuple-element.23), channel_id=1, source_target_pairs={{1,0},{2,1},{3,2},{4,3},{5,4},{6,5},{7,6},{8,7},{9,8},{10,9},{11,1... | collective-permute-start | bytes 12582920 | tf_op jit(solution)/shard_map/ppermute | solution.py:263
  204.2 202.9 %collective-permute-start.1 = (f32[8,128,1024]{2,1,0:T(8,128)}, f32[8,128,1024]{2,1,0:T(8,128)}, u32[]{:S(2)}, u32[]{:S(2)}) collective-permute-start(f32[8,128,1024]{2,1,0:T(8,128)} %get-tuple-element.22), channel_id=1, source_target_pairs={{7,0},{8,1},{9,2},{10,3},{11,4},{12,5},{13,6},{14,7},{15,8},{16,9}... | collective-permute-start | bytes 12582920 | tf_op jit(solution)/shard_map/ppermute | solution.py:263
  407.0 23.2 %copy-start = (f32[128,1024]{1,0:T(8,128)S(1)}, f32[128,1024]{1,0:T(8,128)}, u32[]{:S(2)}) copy-start(f32[128,1024]{1,0:T(8,128)} %get-tuple-element.12) | copy-start | bytes 1572868
where the time goes:
time: 433 us; the launch traced here: 432 us
  waiting for transfers between devices  333 us (77%)
  Pallas kernels  60.3 us (14%)
  local copies, waits for them, and re-layouts  15.6 us (4%)
  starting transfers between devices  11.5 us (3%)
  between operations  8.35 us (2%)
    all_to_all x1, waiting for transfers between devices, on_device(): lax.all_to_all(stored, 'slab', split_axis=0, concat_axis=1, tiled=True)[0]  175 us
    ppermute x2, waiting for transfers between devices, from_behind(): return lax.ppermute(x, axis, pairs)  158 us
    pallas_call x2, Pallas kernels, pair_of(): pl.pallas_call(pair_kernel, out_shape=(jax.ShapeDtypeStruct((across, alon...  40.2 us
    pallas_call x2, Pallas kernels, spectrum_of(): pl.pallas_call(spectrum_kernel, out_shape=(jax.ShapeDtypeStruct((depth, 2...  20.1 us
    dynamic_slice x1, local copies, waits for them, and re-layouts, on_device(): lax.dynamic_slice_in_dim(owned, offsets[rnd, which, 0], A, 1)  12.5 us
  transfers between devices with their start and end apart: 3, of which 2 were waited for; matrix products, arithmetic and copies ran while one was open for 0% of the time, Pallas kernels for 9%

commit v1 on v0

v1 whole, which is shorter than its diff:
```python
import functools
import math

import jax
import jax.numpy as jnp
import numpy as np
from jax import lax
from jax.experimental import pallas as pl
from jax.experimental.pallas import tpu as pltpu
from jax.sharding import PartitionSpec as P

A = 128
GC = 7
ROUNDS = 2
PER_CHIP = 2
FLOOR = 0.25
LANES = 128
F32 = jnp.float32
BF16 = jnp.bfloat16


def halves(table):
    high = table.astype(np.float32).astype(BF16)
    low = (table - high.astype(np.float64)).astype(np.float32).astype(BF16)
    return jnp.asarray(high), jnp.asarray(low)


def phases(rows, cols, total):
    angle = (np.outer(rows, cols) % total) * (2.0 * math.pi / total)
    return np.cos(angle), np.sin(angle)


def make_tables(depth, across, along):
    quarter = along // 4
    half = quarter // 2
    scale = 1.0 / math.sqrt(depth * across * along)
    at = np.arange(quarter)
    cos0, sin0 = phases(at, 4 * np.arange(half), along)
    sin0 = -sin0
    sin0[:, 0] = np.where(at % 2 == 0, 1.0, -1.0)
    first = np.concatenate((cos0, sin0), axis=1) * scale
    cos2, sin2 = phases(at, 4 * np.arange(half) + 2, along)
    second = np.concatenate((cos2, -sin2), axis=1) * scale
    cos1, sin1 = phases(at, 4 * np.arange(quarter) + 1, along)
    third = np.block([[cos1, -sin1], [-sin1, -cos1]]) * scale
    weight = np.full((2 * half, 1), 2.0)
    weight[0] = weight[half] = 1.0
    cos_a, sin_a = phases(np.arange(across), np.arange(across), across)
    rows = np.block([[cos_a, sin_a], [-sin_a, cos_a]])
    cos_z, sin_z = phases(np.arange(depth), np.arange(depth), depth)
    planes = np.zeros((2 * LANES, 2 * LANES))
    planes[:depth, :depth] = cos_z
    planes[:depth, LANES : LANES + depth] = -sin_z
    planes[LANES : LANES + depth, :depth] = sin_z
    planes[LANES : LANES + depth, LANES : LANES + depth] = cos_z
    forth = [first, second, third, rows, planes]
    back = [first.T * weight, second.T * 2.0, third.T * 2.0, rows.T, planes.T]
    flat = lambda group: [part for table in group for part in halves(table)]
    return flat(forth), flat(back)


def split(x):
    high = x.astype(BF16)
    return high, (x - high.astype(F32)).astype(BF16)


def dot(a, b):
    return jnp.dot(a, b, preferred_element_type=F32)


def by_right(x, high, low):
    xh, xl = split(x)
    return dot(xh, high[...]) + (dot(xl, high[...]) + dot(xh, low[...]))


def by_left(high, low, x):
    xh, xl = split(x)
    return dot(high[...], xh) + (dot(high[...], xl) + dot(low[...], xh))


def fft(points, sign):
    n = len(points)
    if n == 1:
        return points
    even = fft(points[0::2], sign)
    odd = fft(points[1::2], sign)
    out = [None] * n
    for k in range(n // 2):
        re, im = odd[k]
        if k == 0:
            pass
        elif 4 * k == n:
            re, im = (-im, re) if sign > 0 else (im, -re)
        elif 8 * k == n:
            r = math.sqrt(0.5)
            re, im = ((re - im) * r, (im + re) * r) if sign > 0 else ((re + im) * r, (im - re) * r)
        elif 8 * k == 3 * n:
            r = math.sqrt(0.5)
            re, im = ((-re - im) * r, (re - im) * r) if sign > 0 else ((im - re) * r, (-im - re) * r)
        else:
            c = math.cos(2.0 * math.pi * k / n)
            s = sign * math.sin(2.0 * math.pi * k / n)
            re, im = re * c - im * s, im * c + re * s
        out[k] = (even[k][0] + re, even[k][1] + im)
        out[k + n // 2] = (even[k][0] - re, even[k][1] - im)
    return out


def whiten(own, partner):
    re = own[0] * partner[0] + own[1] * partner[1]
    im = own[1] * partner[0] - own[0] * partner[1]
    gain = lax.rsqrt(jnp.maximum(re * re + im * im, FLOOR * FLOOR))
    return re * gain, im * gain


def lane_is(shape, lane):
    return lax.broadcasted_iota(jnp.int32, shape, 1) == lane


def spectrum_kernel(slot, count, *refs):
    strips, (f0h, f0l, f2h, f2l, f1h, f1l, rh, rl) = refs[:count], refs[count : count + 8]
    spec, column = refs[count + 8 :]
    depth, across, along = strips[0].shape
    q = along // 4
    h = q // 2
    x = sum(strip[...] for strip in strips).reshape(depth * across, along)
    x0, x1, x2, x3 = (x[:, n * q : (n + 1) * q] for n in range(4))
    s02, s13 = x0 + x2, x1 + x3
    out0 = by_right(s02 + s13, f0h, f0l)
    out2 = by_right(s02 - s13, f2h, f2l)
    out1 = by_right(jnp.concatenate((x0 - x2, x1 - x3), axis=1), f1h, f1l)
    imag0 = out0[:, h:]
    first = lane_is(imag0.shape, 0)
    real = jnp.concatenate((out0[:, :h], out2[:, :h], out1[:, :q]), axis=1)
    imag = jnp.concatenate((jnp.where(first, 0.0, imag0), out2[:, h:], out1[:, q:]), axis=1)
    middles = jnp.zeros(column.shape, F32)
    for n in range(depth):
        rows = slice(n * across, (n + 1) * across)
        spec[n] = by_left(rh, rl, jnp.concatenate((real[rows], imag[rows]), axis=0))
        middle = jnp.broadcast_to(imag0[rows, 0:1], column.shape)
        middles = jnp.where(lane_is(column.shape, slot * depth + n), middle, middles)
    column[...] = middles


def pair_kernel(parts, *refs):
    own, other = refs[:parts], refs[parts : 2 * parts]
    own_cols, other_cols = refs[2 * parts : 3 * parts], refs[3 * parts : 4 * parts]
    (ah, al, zh, zl), back = refs[4 * parts : 4 * parts + 4], refs[4 * parts + 4 : 4 * parts + 14]
    surface, spec, column = refs[4 * parts + 14 :]
    b0h, b0l, b2h, b2l, b1h, b1l, rh, rl, bzh, bzl = back
    per = own[0].shape[0]
    depth = per * parts
    across, along = surface.shape
    q = along // 4
    h = q // 2

    def meet(i, carry):
        re_rows = pl.ds(pl.multiple_of(8 * i, 8), 8)
        im_rows = pl.ds(pl.multiple_of(across + 8 * i, 8), 8)
        for lane in range(0, along // 2, LANES):
            lanes = slice(lane, lane + LANES)
            load = lambda group: [
                (group[z // per][z % per, re_rows, lanes], group[z // per][z % per, im_rows, lanes])
                for z in range(depth)
            ]
            white = [whiten(a, b) for a, b in zip(fft(load(own), -1), fft(load(other), -1))]
            for z, (re, im) in enumerate(fft(white, 1)):
                spec[z, re_rows, lanes] = re
                spec[z, im_rows, lanes] = im
        return carry

    lax.fori_loop(0, across // 8, meet, 0)

    def edge(group):
        turned = by_left(ah.at[:, :across], al.at[:, :across], sum(c[...] for c in group))
        turned = by_right(jnp.concatenate((turned[:across], turned[across:]), axis=1), zh, zl)
        return turned[:, :LANES], turned[:, LANES:]

    white = whiten(edge(own_cols), edge(other_cols))
    back_z = by_right(jnp.concatenate(white, axis=1), bzh, bzl)
    back_z = jnp.concatenate((back_z[:, :LANES], back_z[:, LANES:]), axis=0)
    column[...] = by_left(rh.at[:across], rl.at[:across], back_z)

    surface[...] = jnp.full(surface.shape, -jnp.inf, F32)

    def step(i, carry):
        planes = []
        for n in range(2):
            at = 2 * i + n
            plane = by_left(rh, rl, spec[at])
            middle = jnp.sum(
                jnp.where(lane_is(column.shape, at), column[...], 0.0), axis=1, keepdims=True
            )
            imag0 = plane[across:, :h]
            imag0 = jnp.where(lane_is(imag0.shape, 0), middle, imag0)
            planes.append((plane[:across], imag0, plane[across:, h:]))
        real, imag0, imag = (jnp.concatenate(group, axis=0) for group in zip(*planes))
        z0 = by_right(jnp.concatenate((real[:, :h], imag0), axis=1), b0h, b0l)
        z2 = by_right(jnp.concatenate((real[:, h:q], imag[:, :h]), axis=1), b2h, b2l)
        z1 = by_right(jnp.concatenate((real[:, q:], imag[:, h:]), axis=1), b1h, b1l)
        plus, minus = z0 + z2, z0 - z2
        a, b = z1[:, :q], z1[:, q:]
        for n, part in enumerate((plus + a, minus + b, plus - a, minus - b)):
            lanes = slice(n * q, (n + 1) * q)
            best = jnp.maximum(part[:across], part[across:])
            surface[:, lanes] = jnp.maximum(surface[:, lanes], best)
        return carry

    lax.fori_loop(0, depth // 2, step, 0)


VMEM = pl.BlockSpec(memory_space=pltpu.VMEM)
PARAMS = pltpu.CompilerParams(vmem_limit_bytes=48 * 1024 * 1024)


def spectrum_of(strips, slot, forth):
    depth, across, along = strips[0].shape
    return pl.pallas_call(
        functools.partial(spectrum_kernel, slot, len(strips)),
        out_shape=(
            jax.ShapeDtypeStruct((depth, 2 * across, along // 2), F32),
            jax.ShapeDtypeStruct((across, LANES), F32),
        ),
        in_specs=[VMEM] * (len(strips) + 8),
        out_specs=(VMEM, VMEM),
        compiler_params=PARAMS,
        cost_estimate=pl.CostEstimate(
            flops=2 * 10**9, bytes_accessed=16 * 10**6, transcendentals=0
        ),
    )(*strips, *forth[:8])


def pair_of(own, other, forth, back):
    parts = len(own)
    per, rows, half = own[0][0].shape
    across, along = rows // 2, 2 * half
    operands = [x[0] for x in own] + [x[0] for x in other] + [x[1] for x in own] + [x[1] for x in other]
    operands += forth[6:10] + back
    return pl.pallas_call(
        functools.partial(pair_kernel, parts),
        out_shape=jax.ShapeDtypeStruct((across, along), F32),
        in_specs=[VMEM] * len(operands),
        out_specs=VMEM,
        scratch_shapes=[
            pltpu.VMEM((parts * per, rows, half), F32),
            pltpu.VMEM((across, LANES), F32),
        ],
        compiler_params=PARAMS,
        cost_estimate=pl.CostEstimate(
            flops=12 * 10**9, bytes_accessed=36 * 10**6, transcendentals=0
        ),
    )(*operands)


def on_device(stored, offsets):
    axes = ("tile", "slab")
    slabs = lax.axis_size("slab")
    count = lax.axis_size(axes)
    group = PER_CHIP * slabs
    per, along = stored.shape[1], stored.shape[3]
    forth, back = make_tables(per * slabs, A, along)
    strides = (1, GC)

    def place_of(t):
        inside = t % group
        return (t // group * PER_CHIP + inside % PER_CHIP) * slabs + inside // PER_CHIP

    def giver(rnd, t):
        to = t - strides[rnd]
        return to >= 0 and (rnd == 1 or to % GC != GC - 1)

    def same_slab(rnd, t):
        return place_of(t) % slabs == place_of(t - strides[rnd]) % slabs

    slab = lax.axis_index("slab")
    everyone = lax.all_gather(offsets[:, 1, 0], "slab")
    mine = lax.ppermute(offsets[:, :, 0], axes, [(t, place_of(t)) for t in range(count)])

    def cut(planes, at):
        return lax.dynamic_slice_in_dim(planes, at, A, 1)

    own = [[None] * slabs for _ in range(ROUNDS)]
    other = [[None] * slabs for _ in range(ROUNDS)]
    bands = []
    direct = [[None] * slabs for _ in range(ROUNDS)]
    for step in range(slabs):
        holder = lambda t: t // slabs * slabs + (t - step) % slabs
        which = (slab + step) % slabs
        planes = lax.dynamic_index_in_dim(stored, which, 0, False)
        bands.append(lax.ppermute(planes, axes, [(holder(t), place_of(t)) for t in range(count)]))
        for rnd in range(ROUNDS):
            pairs = [
                (holder(t), place_of(t - strides[rnd]))
                for t in range(count)
                if giver(rnd, t) and not same_slab(rnd, t)
            ]
            at = lax.dynamic_index_in_dim(everyone, which, 0, False)[rnd]
            direct[rnd][step] = lax.ppermute(cut(planes, at), axes, pairs)
    for step in range(slabs):
        slot = slabs - 1 - step
        for rnd in range(ROUNDS):
            own[rnd][slot] = spectrum_of([cut(bands[step], mine[rnd, 0])], slot, forth)
            pairs = [
                (place_of(t), place_of(t - strides[rnd]))
                for t in range(count)
                if giver(rnd, t) and same_slab(rnd, t)
            ]
            near = lax.ppermute(cut(bands[step], mine[rnd, 1]), axes, pairs)
            slot_there = slabs - 1 - (step - strides[rnd]) % slabs
            other[rnd][slot_there] = spectrum_of([near, direct[rnd][step]], slot_there, forth)
    surfaces = []
    for rnd in range(ROUNDS):
        surface = pair_of(own[rnd], other[rnd], forth, back)
        home = lax.ppermute(surface, axes, [(place_of(t), t) for t in range(count)])
        surfaces.append(home)
    surface = jnp.stack(surfaces)[:, None]
    return surface, jnp.max(surface, axis=(2, 3))


def solution(mesh):
    return jax.shard_map(
        on_device,
        mesh=mesh,
        in_specs=(P("tile", "slab", None, None), P(None, None, ("tile", "slab"))),
        out_specs=(P(None, ("tile", "slab"), None, None), P(None, ("tile", "slab"))),
        check_vma=False,
    )
```

time: 433 us -> 420 us (0.970)
  the two profiles are of different devices: /device:TPU:2 before, /device:TPU:28 now
where the time goes in v1:
time: 420 us; the launch traced here: 418 us
  starting transfers between devices  140 us (33%)
  blocking collectives  114 us (27%)
  Pallas kernels  47.7 us (11%)
  local copies, waits for them, and re-layouts  47.2 us (11%)
  waiting for transfers between devices  41.6 us (10%)
  between operations  25.1 us (6%)
    unnamed x1, blocking collectives  114 us
    ppermute x8, starting transfers between devices, on_device(): direct[rnd][step] = lax.ppermute(cut(planes, at), axes, pairs)  60.7 us
    ppermute x8, starting transfers between devices, on_device(): near = lax.ppermute(cut(bands[step], mine[rnd, 1]), axes, pairs)  50.7 us
    ppermute x8, waiting for transfers between devices, on_device(): near = lax.ppermute(cut(bands[step], mine[rnd, 1]), axes, pairs)  30 us
    dynamic_slice x5, local copies, waits for them, and re-layouts, cut(): return lax.dynamic_slice_in_dim(planes, at, A, 1)  26.3 us
    pallas_call x2, Pallas kernels, pair_of(): pl.pallas_call(functools.partial(pair_kernel, parts), out_shape=jax.Shape...  24.1 us
    pallas_call x16, Pallas kernels, spectrum_of(): pl.pallas_call(functools.partial(spectrum_kernel, slot, len(strips)), out...  23.6 us
    ppermute x4, starting transfers between devices, on_device(): lax.ppermute(planes, axes, [(holder(t), place_of(t)) for t in range(count)])  21.3 us
  transfers between devices with their start and end apart: 23, of which 5 were waited for; matrix products, arithmetic and copies ran while one was open for 7% of the time, Pallas kernels for 11%

profile of v1, /device:TPU:28, one launch (start us, length us, event | category | flops | bytes accessed | tf_op | source)
XLA Modules:
  0.0 418.0 jit_solution(7845502926182198501)
XLA Ops:
  0.7 7.5 %dynamic-slice_bitcast_fusion = (f32[2,256,1024]{2,1,0:T(8,128)}, f32[2,256,1024]{2,1,0:T(8,128)}, f32[2,256,1024]{2,1,0:T(8,128)}, f32[2,256,1024]{2,1,0:T(8,128)}) fusion(f32[4,2,256,1024]{3,2,1,0:T(8,128)} %param.22, s32[]{:T(128)S(6)} %select_n.121, s32[]{:T(128)S(6)} %select_n.119, s32[]{:T(128)S(6)} %select_n.117, s32[]{:T(128)S(6)} %select_n.114), kind=kLoop, calls=%fused_computation | loop fusion | bytes 16777232 | tf_op jit(solution)/shard_map/jit(dynamic_index_in_dim)/squeeze | solution.py:289
  8.2 1.9 collective-permute-start.4
  10.1 17.3 %collective-permute-start.3 = (f32[2,256,1024]{2,1,0:T(8,128)}, f32[2,256,1024]{2,1,0:T(8,128)}, u32[]{:S(2)}, u32[]{:S(2)}) collective-permute-start(f32[2,256,1024]{2,1,0:T(8,128)} %get-tuple-element.79), channel_id=1, source_target_pairs={{3,0},{0,4},{1,1},{2,5},{7,2},{4,6},{5,3},{6,7},{11,8},{8,12},{9,9... | collective-permute-start | bytes 6291464 | tf_op jit(solution)/shard_map/ppermute | solution.py:290
  27.5 2.0 collective-permute-start
  31.2 3.7 collective-permute-start.1
  34.9 114.3 %all-reduce = s32[8]{0:T(128)S(1)} all-reduce(s32[8]{0:T(128)S(1)} %dynamic-update-slice), channel_id=2, replica_groups=mesh['tile'=8,'slab'=4] {'slab'}, use_global_device_ids=true, to_apply=%add | all-reduce | flops 8 | bytes 64
  165.7 7.6 %dynamic-slice_bitcast_fusion.8 = (f32[2,128,1024]{2,1,0:T(8,128)}, f32[2,128,1024]{2,1,0:T(8,128)}, f32[2,128,1024]{2,1,0:T(8,128)}, f32[2,128,1024]{2,1,0:T(8,...) fusion(f32[4,2,256,1024]{3,2,1,0:T(8,128)} %param.22, ...), kind=kLoop, calls=%fused_computation.9 | loop fusion | bytes 16777264 | tf_op jit(solution)/shard_map/dynamic_slice | solution.py:280
  173.3 46.2 %collective-permute-start.12 = (f32[2,128,1024]{2,1,0:T(8,128)}, f32[2,128,1024]{2,1,0:T(8,128)S(1)}, u32[]{:S(2)}, u32[]{:S(2)}) collective-permute-start(f32[2,128,1024]{2,1,0:T(8,128)} %get-tuple-element.70), channel_id=1, source_target_pairs={{1,4},{7,5},{5,6},{11,7},{9,12},{15,13},{19,15},{17,20},{23,21},{2... | collective-permute-start | bytes 3145736 | tf_op jit(solution)/shard_map/ppermute | solution.py:298
  228.6 4.7 %constant_dynamic-slice_fusion.15 = (f32[2,128,1024]{2,1,0:T(8,128)}, f32[2,128,1024]{2,1,0:T(8,128)}, f32[2,128,1024]{2,1,0:T(8,128)S(1)}, f32[2,128,1024]{2,1,0:T(8,128)S(1)}) fusion(f32[2,256,1024]{2,1,0:T(8,128)} %collective-permute-done.4, s32[]{:T(128)S(6)} %select_n.122, s32[]{:T(128)S(6)} %select_n.136, s32[]{:T(128)S(6)} %select_n.135, s32[]{:T(128)S(6)} %select_n.115), kind=kLoop, calls=%fused_computation.30 | loop fusion | bytes 8388624 | tf_op jit(solution)/shard_map/dynamic_slice | solution.py:280
  234.7 1.9 collective-permute-start.19
  236.6 4.7 %constant_dynamic-slice_fusion.9 = (f32[2,128,1024]{2,1,0:T(8,128)}, f32[2,128,1024]{2,1,0:T(8,128)}, f32[2,128,1024]{2,1,0:T(8,128)S(1)}, f32[2,128,1024]{2,1,0:T(8,128)S(1)}) fusion(f32[2,256,1024]{2,1,0:T(8,128)} %collective-permute-done.3, s32[]{:T(128)S(6)} %select_n.122, s32[]{:T(128)S(6)} %select_n.136, s32[]{:T(128)S(6)} %select_n.135, s32[]{:T(128)S(6)} %select_n.115), kind=kLoop, calls=%fused_computation.24 | loop fusion | bytes 8388624 | tf_op jit(solution)/shard_map/dynamic_slice | solution.py:280
  244.0 6.8 %collective-permute-start.18 = (f32[2,128,1024]{2,1,0:T(8,128)}, f32[2,128,1024]{2,1,0:T(8,128)S(1)}, u32[]{:S(2)}, u32[]{:S(2)}) collective-permute-start(f32[2,128,1024]{2,1,0:T(8,128)} %get-tuple-element.95), channel_id=1, source_target_pairs={{8,4},{9,5},{10,6},{11,7},{16,12},{17,13},{18,14},{19,15},{24,20},... | collective-permute-start | bytes 3145736 | tf_op jit(solution)/shard_map/ppermute | solution.py:308
  256.8 4.6 %constant_dynamic-slice_fusion.11 = (f32[2,128,1024]{2,1,0:T(8,128)}, f32[2,128,1024]{2,1,0:T(8,128)}, f32[2,128,1024]{2,1,0:T(8,128)S(1)}, f32[2,128,1024]{2,1,0:T(8,128)S(1)}) fusion(f32[2,256,1024]{2,1,0:T(8,128)} %collective-permute-done.2, s32[]{:T(128)S(6)} %select_n.122, s32[]{:T(128)S(6)} %select_n.136, s32[]{:T(128)S(6)} %select_n.135, s32[]{:T(128)S(6)} %select_n.115), kind=kLoop, calls=%fused_computation.26 | loop fusion | bytes 8388624 | tf_op jit(solution)/shard_map/dynamic_slice | solution.py:280
  262.7 4.6 %constant_dynamic-slice_fusion.13 = (f32[2,128,1024]{2,1,0:T(8,128)S(1)}, f32[2,128,1024]{2,1,0:T(8,128)}, f32[2,128,1024]{2,1,0:T(8,128)S(1)}, f32[2,128,1024]{2,1,0:T(8,128)S(1)}) fusion(f32[2,256,1024]{2,1,0:T(8,128)} %copy-done.51, s32[]{:T(128)S(6)} %select_n.122, s32[]{:T(128)S(6)} %select_n.136, s32[]{:T(128)S(6)} %select_n.135, s32[]{:T(128)S(6)} %select_n.115), kind=kLoop, calls=%fused_computation.28 | loop fusion | bytes 8388624 | tf_op jit(solution)/shard_map/dynamic_slice | solution.py:280
  268.1 1.5 collective-permute-start.9
  271.9 6.4 %collective-permute-start.8 = (f32[2,128,1024]{2,1,0:T(8,128)}, f32[2,128,1024]{2,1,0:T(8,128)S(1)}, u32[]{:S(2)}, u32[]{:S(2)}) collective-permute-start(f32[2,128,1024]{2,1,0:T(8,128)} %get-tuple-element.74), channel_id=1, source_target_pairs={{3,4},{5,5},{7,6},{9,7},{11,12},{13,13},{17,15},{19,20},{21,21},{2... | collective-permute-start | bytes 3145736 | tf_op jit(solution)/shard_map/ppermute | solution.py:298
  290.7 1.9 collective-permute-start.15
  292.7 1.4 collective-permute-start.21
  294.1 2.6 shard_map.227
  297.7 2.1 collective-permute-done.8.refs_1_
  299.9 35.5 %collective-permute-start.16 = (f32[2,128,1024]{2,1,0:T(8,128)}, f32[2,128,1024]{2,1,0:T(8,128)S(1)}, u32[]{:S(2)}, u32[]{:S(2)}) collective-permute-start(f32[2,128,1024]{2,1,0:T(8,128)} %get-tuple-element.83), channel_id=1, source_target_pairs={{8,4},{9,5},{10,6},{11,7},{16,12},{17,13},{18,14},{19,15},{24,20},... | collective-permute-start | bytes 3145736 | tf_op jit(solution)/shard_map/ppermute | solution.py:308
  335.6 1.7 collective-permute-start.14
  337.3 2.6 shard_map.226
  343.6 12.0 %shard_map.229 = f32[128,1024]{1,0:T(8,128)S(1)} custom-call(f32[2,256,512]{2,1,0:T(8,128)S(1)} %copy-done.42, f32[2,256,512]{2,1,0:T(8,128)S(1)} %copy-done.40, f32[2,256,512]{2,1,0:T(8,128)} %copy-done.38, f32[2,256,512]{2,1,0:T(8,128)} %copy-done.35, f32[2,256,512]{2,1,0:T(8,128)} %copy-done.24, f32[2,256,512]{2,1,0:T(8,128)} %copy-done.30, ...), custom_call_target="tpu_custom_call" | custom-call | flops 12000000000 | bytes 36000000 | tf_op jit(solution)/shard_map/pallas_call | solution.py:239
  355.6 12.5 %collective-permute-done.16.refs_0_ = f32[2,128,1024]{2,1,0:T(8,128)S(1)} collective-permute-done((f32[2,128,1024]{2,1,0:T(8,128)}, f32[2,128,1024]{2,1,0:T(8,128)S(1)}, u32[]{:S(2)}, u32[]{:S(2)}) %collective-permute-start.16) | collective-permute-done | bytes 1048608 | tf_op jit(solution)/shard_map/ppermute | solution.py:308
  368.2 2.1 collective-permute-start.13
  371.7 7.7 %collective-permute-done.14.refs_0_ = f32[2,128,1024]{2,1,0:T(8,128)S(1)} collective-permute-done((f32[2,128,1024]{2,1,0:T(8,128)}, f32[2,128,1024]{2,1,0:T(8,128)S(1)}, u32[]{:S(2)}, u32[]{:S(2)}) %collective-permute-start.14) | collective-permute-done | bytes 1048608 | tf_op jit(solution)/shard_map/ppermute | solution.py:308
  380.8 9.7 %collective-permute-done.20.refs_0_ = f32[2,128,1024]{2,1,0:T(8,128)S(1)} collective-permute-done((f32[2,128,1024]{2,1,0:T(8,128)S(1)}, f32[2,128,1024]{2,1,0:T(8,128)S(1)}, u32[]{:S(2)}, u32[]{:S(2)}) %collective-permute-start.20) | collective-permute-done | bytes 1048608 | tf_op jit(solution)/shard_map/ppermute | solution.py:308
  392.9 12.1 %shard_map.238 = f32[128,1024]{1,0:T(8,128)S(1)} custom-call(f32[2,256,512]{2,1,0:T(8,128)S(1)} %copy-done.37, f32[2,256,512]{2,1,0:T(8,128)S(1)} %copy-done.34, f32[2,256,512]{2,1,0:T(8,128)} %copy-done.32, f32[2,256,512]{2,1,0:T(8,128)} %copy-done.31, f32[2,256,512]{2,1,0:T(8,128)} %copy-done.27, f32[2,256,512]{2,1,0:T(8,128)} %copy-done.26, ...), custom_call_target="tpu_custom_call" | custom-call | flops 12000000000 | bytes 36000000 | tf_op jit(solution)/shard_map/pallas_call | solution.py:239
  405.0 1.9 collective-permute-start.22
  406.9 9.5 %collective-permute-done.22 = f32[128,1024]{1,0:T(8,128)S(1)} collective-permute-done((f32[128,1024]{1,0:T(8,128)S(1)}, f32[128,1024]{1,0:T(8,128)S(1)}, u32[]{:S(2)}, u32[]{:S(2)}) %collective-permute-start.22) | collective-permute-done | bytes 524320 | tf_op jit(solution)/shard_map/ppermute | solution.py:314
  416.4 1.6 fusion
  (161 shorter events, 40.1 us)
Async XLA Ops:
  0.7 28.8 %copy-start.55 = (u32[32]{0:T(128)S(1)}, u32[32]{0:T(128)}, u32[]{:S(2)}) copy-start(u32[32]{0:T(128)} %constant.292) | copy-start | bytes 388
  0.7 30.0 %copy-start.54 = (s32[2,2,1]{1,2,0:T(1,128)S(1)}, s32[2,2,1]{1,2,0:T(1,128)}, u32[]{:S(2)}) copy-start(s32[2,2,1]{1,2,0:T(1,128)} %param.23) | copy-start | bytes 52
  8.2 219.4 %collective-permute-start.4 = (f32[2,256,1024]{2,1,0:T(8,128)}, f32[2,256,1024]{2,1,0:T(8,128)}, u32[]{:S(2)}, u32[]{:S(2)}) collective-permute-start(f32[2,256,1024]{2,1,0:T(8,128)} %get-tuple-element.78), channel_id=1, source_target_pairs={{0,0},{1,4},{2,1},{3,5},{4,2},{5,6},{6,3},{7,7},{8,8},{9,12},{10,9... | collective-permute-start | bytes 6291464 | tf_op jit(solution)/shard_map/ppermute | solution.py:290
  10.1 224.6 %collective-permute-start.3 = (f32[2,256,1024]{2,1,0:T(8,128)}, f32[2,256,1024]{2,1,0:T(8,128)}, u32[]{:S(2)}, u32[]{:S(2)}) collective-permute-start(f32[2,256,1024]{2,1,0:T(8,128)} %get-tuple-element.79), channel_id=1, source_target_pairs={{3,0},{0,4},{1,1},{2,5},{7,2},{4,6},{5,3},{6,7},{11,8},{8,12},{9,9... | collective-permute-start | bytes 6291464 | tf_op jit(solution)/shard_map/ppermute | solution.py:290
  27.5 216.6 %collective-permute-start.2 = (f32[2,256,1024]{2,1,0:T(8,128)}, f32[2,256,1024]{2,1,0:T(8,128)}, u32[]{:S(2)}, u32[]{:S(2)}) collective-permute-start(f32[2,256,1024]{2,1,0:T(8,128)} %get-tuple-element.80), channel_id=1, source_target_pairs={{2,0},{3,4},{0,1},{1,5},{6,2},{7,6},{4,3},{5,7},{10,8},{11,12},{8,... | collective-permute-start | bytes 6291464 | tf_op jit(solution)/shard_map/ppermute | solution.py:290
  27.5 225.7 %collective-permute-start = (f32[2,256,1024]{2,1,0:T(8,128)}, f32[2,256,1024]{2,1,0:T(8,128)S(1)}, u32[]{:S(2)}, u32[]{:S(2)}) collective-permute-start(f32[2,256,1024]{2,1,0:T(8,128)} %get-tuple-element.81), channel_id=1, source_target_pairs={{1,0},{2,4},{3,1},{0,5},{5,2},{6,6},{7,3},{4,7},{9,8},{10,12},{11,... | collective-permute-start | bytes 6291464 | tf_op jit(solution)/shard_map/ppermute | solution.py:290
  31.2 142.1 %collective-permute-start.1 = (s32[2,2]{1,0:T(2,128)S(1)}, s32[2,2]{1,0:T(2,128)S(1)}, u32[]{:S(2)}, u32[]{:S(2)}) collective-permute-start(s32[2,2]{1,0:T(2,128)S(1)} %bitcast.48), channel_id=1, source_target_pairs={{0,0},{1,4},{2,1},{3,5},{4,2},{5,6},{6,3},{7,7},{8,8},{9,12},{10,9... | collective-permute-start | bytes 56 | tf_op jit(solution)/shard_map/ppermute | solution.py:277
  173.3 69.4 %collective-permute-start.12 = (f32[2,128,1024]{2,1,0:T(8,128)}, f32[2,128,1024]{2,1,0:T(8,128)S(1)}, u32[]{:S(2)}, u32[]{:S(2)}) collective-permute-start(f32[2,128,1024]{2,1,0:T(8,128)} %get-tuple-element.70), channel_id=1, source_target_pairs={{1,4},{7,5},{5,6},{11,7},{9,12},{15,13},{19,15},{17,20},{23,21},{2... | collective-permute-start | bytes 3145736 | tf_op jit(solution)/shard_map/ppermute | solution.py:298
  227.7 39.6 %collective-permute-start.6 = (f32[2,128,1024]{2,1,0:T(8,128)}, f32[2,128,1024]{2,1,0:T(8,128)S(1)}, u32[]{:S(2)}, u32[]{:S(2)}) collective-permute-start(f32[2,128,1024]{2,1,0:T(8,128)} %get-tuple-element.75), channel_id=1, source_target_pairs={{2,4},{4,5},{6,6},{8,7},{10,12},{12,13},{16,15},{18,20},{20,21},{2... | collective-permute-start | bytes 3145736 | tf_op jit(solution)/shard_map/ppermute | solution.py:298
  234.7 33.4 %collective-permute-start.19 = (f32[2,128,1024]{2,1,0:T(8,128)}, f32[2,128,1024]{2,1,0:T(8,128)S(1)}, u32[]{:S(2)}, u32[]{:S(2)}) collective-permute-start(f32[2,128,1024]{2,1,0:T(8,128)} %get-tuple-element.77), channel_id=1, source_target_pairs={{7,0},{9,1},{11,2},{13,3},{15,8},{17,9},{19,10},{21,11},{23,16},{2... | collective-permute-start | bytes 3145736 | tf_op jit(solution)/shard_map/ppermute | solution.py:298
  242.7 29.2 %collective-permute-start.5 = (f32[2,128,1024]{2,1,0:T(8,128)}, f32[2,128,1024]{2,1,0:T(8,128)S(1)}, u32[]{:S(2)}, u32[]{:S(2)}) collective-permute-start(f32[2,128,1024]{2,1,0:T(8,128)} %get-tuple-element.94), channel_id=1, source_target_pairs={{4,0},{5,1},{6,2},{12,8},{13,9},{14,10},{15,11},{20,16},{21,17},{2... | collective-permute-start | bytes 3145736 | tf_op jit(solution)/shard_map/ppermute | solution.py:308
  244.0 34.4 %collective-permute-start.18 = (f32[2,128,1024]{2,1,0:T(8,128)}, f32[2,128,1024]{2,1,0:T(8,128)S(1)}, u32[]{:S(2)}, u32[]{:S(2)}) collective-permute-start(f32[2,128,1024]{2,1,0:T(8,128)} %get-tuple-element.95), channel_id=1, source_target_pairs={{8,4},{9,5},{10,6},{11,7},{16,12},{17,13},{18,14},{19,15},{24,20},... | collective-permute-start | bytes 3145736 | tf_op jit(solution)/shard_map/ppermute | solution.py:308
  253.2 28.8 %collective-permute-start.11 = (f32[2,128,1024]{2,1,0:T(8,128)}, f32[2,128,1024]{2,1,0:T(8,128)S(1)}, u32[]{:S(2)}, u32[]{:S(2)}) collective-permute-start(f32[2,128,1024]{2,1,0:T(8,128)} %get-tuple-element.82), channel_id=1, source_target_pairs={{4,0},{5,1},{6,2},{12,8},{13,9},{14,10},{15,11},{20,16},{21,17},{2... | collective-permute-start | bytes 3145736 | tf_op jit(solution)/shard_map/ppermute | solution.py:308
  267.3 23.3 %collective-permute-start.10 = (f32[2,128,1024]{2,1,0:T(8,128)}, f32[2,128,1024]{2,1,0:T(8,128)S(1)}, u32[]{:S(2)}, u32[]{:S(2)}) collective-permute-start(f32[2,128,1024]{2,1,0:T(8,128)} %get-tuple-element.73), channel_id=1, source_target_pairs={{0,4},{6,5},{4,6},{10,7},{8,12},{14,13},{18,15},{16,20},{22,21},{2... | collective-permute-start | bytes 3145736 | tf_op jit(solution)/shard_map/ppermute | solution.py:298
  268.1 24.5 %collective-permute-start.9 = (f32[2,128,1024]{2,1,0:T(8,128)}, f32[2,128,1024]{2,1,0:T(8,128)}, u32[]{:S(2)}, u32[]{:S(2)}) collective-permute-start(f32[2,128,1024]{2,1,0:T(8,128)} %get-tuple-element.86), channel_id=1, source_target_pairs={{4,0},{5,1},{6,2},{12,8},{13,9},{14,10},{15,11},{20,16},{21,17},{2... | collective-permute-start | bytes 3145736 | tf_op jit(solution)/shard_map/ppermute | solution.py:308
  269.6 10.1 %copy-start.5 = (bf16[512,512]{1,0:T(8,128)(2,1)S(1)}, bf16[512,512]{1,0:T(8,128)(2,1)}, u32[]{:S(2)}) copy-start(bf16[512,512]{1,0:T(8,128)(2,1)} %constant.272.clone.refs_5_.refs_6_) | copy-start | bytes 1572868
  271.9 27.9 %collective-permute-start.8 = (f32[2,128,1024]{2,1,0:T(8,128)}, f32[2,128,1024]{2,1,0:T(8,128)S(1)}, u32[]{:S(2)}, u32[]{:S(2)}) collective-permute-start(f32[2,128,1024]{2,1,0:T(8,128)} %get-tuple-element.74), channel_id=1, source_target_pairs={{3,4},{5,5},{7,6},{9,7},{11,12},{13,13},{17,15},{19,20},{21,21},{2... | collective-permute-start | bytes 3145736 | tf_op jit(solution)/shard_map/ppermute | solution.py:298
  278.4 57.0 %collective-permute-start.7 = (f32[2,128,1024]{2,1,0:T(8,128)S(1)}, f32[2,128,1024]{2,1,0:T(8,128)}, u32[]{:S(2)}, u32[]{:S(2)}) collective-permute-start(f32[2,128,1024]{2,1,0:T(8,128)S(1)} %get-tuple-element.90), channel_id=1, source_target_pairs={{4,0},{5,1},{6,2},{12,8},{13,9},{14,10},{15,11},{20,16},{21,17},{2... | collective-permute-start | bytes 3145736 | tf_op jit(solution)/shard_map/ppermute | solution.py:308
  282.0 58.8 %collective-permute-start.17 = (f32[2,128,1024]{2,1,0:T(8,128)}, f32[2,128,1024]{2,1,0:T(8,128)S(1)}, u32[]{:S(2)}, u32[]{:S(2)}) collective-permute-start(f32[2,128,1024]{2,1,0:T(8,128)} %get-tuple-element.71), channel_id=1, source_target_pairs={{6,0},{8,1},{10,2},{12,3},{14,8},{16,9},{18,10},{20,11},{22,16},{2... | collective-permute-start | bytes 3145736 | tf_op jit(solution)/shard_map/ppermute | solution.py:298
  290.7 81.0 %collective-permute-start.15 = (f32[2,128,1024]{2,1,0:T(8,128)}, f32[2,128,1024]{2,1,0:T(8,128)S(1)}, u32[]{:S(2)}, u32[]{:S(2)}) collective-permute-start(f32[2,128,1024]{2,1,0:T(8,128)} %get-tuple-element.72), channel_id=1, source_target_pairs={{5,0},{11,1},{9,2},{15,3},{13,8},{19,9},{17,10},{23,11},{21,16},{2... | collective-permute-start | bytes 3145736 | tf_op jit(solution)/shard_map/ppermute | solution.py:298
  292.7 44.7 %copy-start.3 = (bf16[512,512]{1,0:T(8,128)(2,1)S(1)}, bf16[512,512]{1,0:T(8,128)(2,1)}, u32[]{:S(2)}) copy-start(bf16[512,512]{1,0:T(8,128)(2,1)} %constant.273.clone.refs_6_.refs_7_) | copy-start | bytes 1572868
  292.7 88.2 %collective-permute-start.21 = (f32[2,128,1024]{2,1,0:T(8,128)S(1)}, f32[2,128,1024]{2,1,0:T(8,128)S(1)}, u32[]{:S(2)}, u32[]{:S(2)}) collective-permute-start(f32[2,128,1024]{2,1,0:T(8,128)S(1)} %copy-done.52), channel_id=1, source_target_pairs={{4,0},{10,1},{8,2},{14,3},{12,8},{18,9},{16,10},{22,11},{20,16},{2... | collective-permute-start | bytes 3145736 | tf_op jit(solution)/shard_map/ppermute | solution.py:298
  299.9 68.3 %collective-permute-start.16 = (f32[2,128,1024]{2,1,0:T(8,128)}, f32[2,128,1024]{2,1,0:T(8,128)S(1)}, u32[]{:S(2)}, u32[]{:S(2)}) collective-permute-start(f32[2,128,1024]{2,1,0:T(8,128)} %get-tuple-element.83), channel_id=1, source_target_pairs={{8,4},{9,5},{10,6},{11,7},{16,12},{17,13},{18,14},{19,15},{24,20},... | collective-permute-start | bytes 3145736 | tf_op jit(solution)/shard_map/ppermute | solution.py:308
  335.6 43.8 %collective-permute-start.14 = (f32[2,128,1024]{2,1,0:T(8,128)}, f32[2,128,1024]{2,1,0:T(8,128)S(1)}, u32[]{:S(2)}, u32[]{:S(2)}) collective-permute-start(f32[2,128,1024]{2,1,0:T(8,128)} %get-tuple-element.87), channel_id=1, source_target_pairs={{8,4},{9,5},{10,6},{11,7},{16,12},{17,13},{18,14},{19,15},{24,20},... | collective-permute-start | bytes 3145736 | tf_op jit(solution)/shard_map/ppermute | solution.py:308
  340.9 49.7 %collective-permute-start.20 = (f32[2,128,1024]{2,1,0:T(8,128)S(1)}, f32[2,128,1024]{2,1,0:T(8,128)S(1)}, u32[]{:S(2)}, u32[]{:S(2)}) collective-permute-start(f32[2,128,1024]{2,1,0:T(8,128)S(1)} %copy-done.53), channel_id=1, source_target_pairs={{8,4},{9,5},{10,6},{11,7},{16,12},{17,13},{18,14},{19,15},{24,20},... | collective-permute-start | bytes 3145736 | tf_op jit(solution)/shard_map/ppermute | solution.py:308
  368.2 38.7 %collective-permute-start.13 = (f32[128,1024]{1,0:T(8,128)S(1)}, f32[128,1024]{1,0:T(8,128)S(1)}, u32[]{:S(2)}, u32[]{:S(2)}) collective-permute-start(f32[128,1024]{1,0:T(8,128)S(1)} %shard_map.229), channel_id=1, source_target_pairs={{0,0},{4,1},{1,2},{5,3},{2,4},{6,5},{3,6},{7,7},{8,8},{12,9},{9,10... | collective-permute-start | bytes 1572872 | tf_op jit(solution)/shard_map/ppermute | solution.py:314
  380.8 11.1 %copy-start.27 = (f32[2,256,512]{2,1,0:T(8,128)}, f32[2,256,512]{2,1,0:T(8,128)S(1)}, u32[]{:S(2)}) copy-start(f32[2,256,512]{2,1,0:T(8,128)S(1)} %get-tuple-element.54.refs_4_) | copy-start | bytes 3145732
  380.8 12.1 %copy-start.34 = (f32[2,256,512]{2,1,0:T(8,128)S(1)}, f32[2,256,512]{2,1,0:T(8,128)}, u32[]{:S(2)}) copy-start(f32[2,256,512]{2,1,0:T(8,128)} %copy-done.33) | copy-start | bytes 3145732
  380.8 12.1 %copy-start.37 = (f32[2,256,512]{2,1,0:T(8,128)S(1)}, f32[2,256,512]{2,1,0:T(8,128)}, u32[]{:S(2)}) copy-start(f32[2,256,512]{2,1,0:T(8,128)} %copy-done.36) | copy-start | bytes 3145732
  380.8 12.1 %copy-start.44 = (f32[128,128]{1,0:T(8,128)S(1)}, f32[128,128]{1,0:T(8,128)}, u32[]{:S(2)}) copy-start(f32[128,128]{1,0:T(8,128)} %copy-done.43) | copy-start | bytes 196612
  380.8 12.1 %copy-start.48 = (f32[128,128]{1,0:T(8,128)S(1)}, f32[128,128]{1,0:T(8,128)}, u32[]{:S(2)}) copy-start(f32[128,128]{1,0:T(8,128)} %copy-done.47) | copy-start | bytes 196612
  405.0 11.4 %collective-permute-start.22 = (f32[128,1024]{1,0:T(8,128)S(1)}, f32[128,1024]{1,0:T(8,128)S(1)}, u32[]{:S(2)}, u32[]{:S(2)}) collective-permute-start(f32[128,1024]{1,0:T(8,128)S(1)} %shard_map.238), channel_id=1, source_target_pairs={{0,0},{4,1},{1,2},{5,3},{2,4},{6,5},{3,6},{7,7},{8,8},{12,9},{9,10... | collective-permute-start | bytes 1572872 | tf_op jit(solution)/shard_map/ppermute | solution.py:314
  (47 other events, 232.2 us)

commit v2 on v1

--- a/solution.py
+++ b/solution.py
@@ -265,55 +265,72 @@
         inside = t % group
         return (t // group * PER_CHIP + inside % PER_CHIP) * slabs + inside // PER_CHIP
 
-    def giver(rnd, t):
+    def gives(rnd, t):
         to = t - strides[rnd]
         return to >= 0 and (rnd == 1 or to % GC != GC - 1)
 
-    def same_slab(rnd, t):
-        return place_of(t) % slabs == place_of(t - strides[rnd]) % slabs
-
-    slab = lax.axis_index("slab")
-    everyone = lax.all_gather(offsets[:, 1, 0], "slab")
-    mine = lax.ppermute(offsets[:, :, 0], axes, [(t, place_of(t)) for t in range(count)])
+    def holder(t, step, of):
+        return t // slabs * slabs + (of - step) % slabs
+
+    near = [(t, t - strides[1 - t % 2]) for t in range(count) if gives(1 - t % 2, t)]
+    far = [(t, t - strides[t % 2]) for t in range(count) if gives(t % 2, t)]
+
+    tile, slab = lax.axis_index("tile"), lax.axis_index("slab")
+    here = tile // PER_CHIP * group + slab * PER_CHIP + tile % PER_CHIP
+    odd = here % 2
+    table = lax.all_gather(offsets[:, :, 0], axes)
+    stored, table = lax.optimization_barrier((stored, table))
 
     def cut(planes, at):
         return lax.dynamic_slice_in_dim(planes, at, A, 1)
 
-    own = [[None] * slabs for _ in range(ROUNDS)]
-    other = [[None] * slabs for _ in range(ROUNDS)]
-    bands = []
-    direct = [[None] * slabs for _ in range(ROUNDS)]
+    bands, fars = [], []
     for step in range(slabs):
-        holder = lambda t: t // slabs * slabs + (t - step) % slabs
-        which = (slab + step) % slabs
+        planes = lax.dynamic_index_in_dim(stored, (slab + step) % slabs, 0, False)
+        bands.append(
+            lax.ppermute(planes, axes, [(holder(t, step, t), place_of(t)) for t in range(count)])
+        )
+        ahead = (slab + step) % slabs
+        which = jnp.where(
+            (ahead + strides[0]) % 2 == 0, (ahead + strides[0]) % slabs, (ahead + strides[1]) % slabs
+        )
         planes = lax.dynamic_index_in_dim(stored, which, 0, False)
-        bands.append(lax.ppermute(planes, axes, [(holder(t), place_of(t)) for t in range(count)]))
-        for rnd in range(ROUNDS):
-            pairs = [
-                (holder(t), place_of(t - strides[rnd]))
-                for t in range(count)
-                if giver(rnd, t) and not same_slab(rnd, t)
-            ]
-            at = lax.dynamic_index_in_dim(everyone, which, 0, False)[rnd]
-            direct[rnd][step] = lax.ppermute(cut(planes, at), axes, pairs)
-    for step in range(slabs):
-        slot = slabs - 1 - step
-        for rnd in range(ROUNDS):
-            own[rnd][slot] = spectrum_of([cut(bands[step], mine[rnd, 0])], slot, forth)
-            pairs = [
-                (place_of(t), place_of(t - strides[rnd]))
-                for t in range(count)
-                if giver(rnd, t) and same_slab(rnd, t)
-            ]
-            near = lax.ppermute(cut(bands[step], mine[rnd, 1]), axes, pairs)
-            slot_there = slabs - 1 - (step - strides[rnd]) % slabs
-            other[rnd][slot_there] = spectrum_of([near, direct[rnd][step]], slot_there, forth)
-    surfaces = []
-    for rnd in range(ROUNDS):
-        surface = pair_of(own[rnd], other[rnd], forth, back)
-        home = lax.ppermute(surface, axes, [(place_of(t), t) for t in range(count)])
-        surfaces.append(home)
-    surface = jnp.stack(surfaces)[:, None]
+        at = table[tile * slabs + which, which % 2, 1]
+        fars.append(
+            lax.ppermute(
+                cut(planes, at), axes, [(holder(t, step, to), place_of(to)) for t, to in far]
+            )
+        )
+
+    def spectra(pieces):
+        return [spectrum_of([piece], n, forth) for n, piece in enumerate(pieces[::-1])]
+
+    def own(rnd):
+        at = table[here, rnd, 0]
+        return spectra([cut(band, at) for band in bands])
+
+    def surface_of(rnd, arrived):
+        surface = pair_of(own(rnd), spectra(arrived), forth, back)
+        return lax.ppermute(surface, axes, [(place_of(t), t) for t in range(count)])
+
+    given = [cut(band, table[here, 1 - odd, 1]) for band in bands]
+    nears = [None] * slabs
+    for first in (1, 0):
+        steps = range(first, slabs, 2)
+        ready = [
+            jnp.where(odd == 1, given[(s + strides[0]) % slabs], given[(s + strides[1]) % slabs])
+            for s in steps
+        ]
+        pairs = [(place_of(t), place_of(to)) for t, to in near]
+        arrived = lax.ppermute(jnp.concatenate(ready), axes, pairs)
+        for n, s in enumerate(steps):
+            nears[s] = arrived[n * per : (n + 1) * per]
+    from_far = surface_of(1 - odd, fars)
+    from_near = surface_of(odd, nears)
+    home_odd = (tile * slabs + slab) % 2 == 1
+    surface = jnp.stack(
+        (jnp.where(home_odd, from_far, from_near), jnp.where(home_odd, from_near, from_far))
+    )[:, None]
     return surface, jnp.max(surface, axis=(2, 3))
 
 

time: 420 us -> 455 us (1.083)
  waiting for transfers between devices: 41.6 us -> 147 us
  blocking collectives: 114 us -> 60.5 us
  other arithmetic: 1.63 us -> 18.1 us
  local copies, waits for them, and re-layouts: 47.2 us -> 32.4 us
  between operations: 25.1 us -> 15.2 us
  starting transfers between devices: 140 us -> 134 us
    unnamed x1 -> x0, blocking collectives: 114 us -> none
    ppermute x23 -> x12, waiting for transfers between devices: 41.6 us -> 147 us  [the longest x4 69.2 us: on_device(): lax.ppermute(cut(planes, at), axes, [(holder(t, step, to), place_of(to))...]
    all_gather x0 -> x1, blocking collectives: none -> 60.5 us  [on_device(): table = lax.all_gather(offsets[:, :, 0], axes)]
    dynamic_slice x5 -> x1, local copies, waits for them, and re-layouts: 26.3 us -> 4.91 us  [cut(): return lax.dynamic_slice_in_dim(planes, at, A, 1)]
    select_n x0 -> x1, other arithmetic: none -> 10.5 us  [on_device(): jnp.where(odd == 1, given[(s + strides[0]) % slabs], given[(s + strides[1...]
    ppermute x23 -> x12, starting transfers between devices: 140 us -> 134 us  [the longest x2 52.2 us: surface_of(): return lax.ppermute(surface, axes, [(place_of(t), t) for t in range(count)])]
    concatenate x0 -> x2, other arithmetic: none -> 4.86 us  [on_device(): arrived = lax.ppermute(jnp.concatenate(ready), axes, pairs)]
    unnamed x115 -> x102, local copies, waits for them, and re-layouts: 11.2 us -> 15 us
  transfers between devices with their start and end apart: 23 -> 12, of which waited for: 5 -> 4; matrix products, arithmetic and copies ran while one was open for 7% -> 3% of each run, Pallas kernels for 11% -> 10%
where the time goes in v2:
time: 455 us; the launch traced here: 453 us
  waiting for transfers between devices  147 us (32%)
  starting transfers between devices  134 us (29%)
  blocking collectives  60.5 us (13%)
  Pallas kernels  46.3 us (10%)
  local copies, waits for them, and re-layouts  32.4 us (7%)
  other arithmetic  18.1 us (4%)
  between operations  15.2 us (3%)
    ppermute x4, waiting for transfers between devices, on_device(): lax.ppermute(cut(planes, at), axes, [(holder(t, step, to), place_of(to))...  69.2 us
    ppermute x4, waiting for transfers between devices, on_device(): lax.ppermute(planes, axes, [(holder(t, step, t), place_of(t)) for t in ra...  68 us
    all_gather x1, blocking collectives, on_device(): table = lax.all_gather(offsets[:, :, 0], axes)  60.5 us
    ppermute x2, starting transfers between devices, surface_of(): return lax.ppermute(surface, axes, [(place_of(t), t) for t in range(count)])  52.2 us
    ppermute x4, starting transfers between devices, on_device(): lax.ppermute(cut(planes, at), axes, [(holder(t, step, to), place_of(to))...  46.3 us
    ppermute x4, starting transfers between devices, on_device(): lax.ppermute(planes, axes, [(holder(t, step, t), place_of(t)) for t in ra...  31.3 us
    pallas_call x2, Pallas kernels, pair_of(): pl.pallas_call(functools.partial(pair_kernel, parts), out_shape=jax.Shape...  24.2 us
    pallas_call x16, Pallas kernels, spectrum_of(): pl.pallas_call(functools.partial(spectrum_kernel, slot, len(strips)), out...  22.1 us
  transfers between devices with their start and end apart: 12, of which 4 were waited for; matrix products, arithmetic and copies ran while one was open for 3% of the time, Pallas kernels for 10%

profile of v2, /device:TPU:28, one launch (start us, length us, event | category | flops | bytes accessed | tf_op | source)
XLA Modules:
  0.0 453.2 jit_solution(467845520097663355)
XLA Ops:
  1.0 60.5 %all-gather = s32[64,2,1]{1,2,0:T(1,128)S(1)} all-gather(s32[2,2,1]{1,2,0:T(1,128)} %param.23), channel_id=2, replica_groups=mesh['tile'=8,'slab'=4] {'tile','slab'}, dimensions={0}, use_global_device_ids=true | all-gather | bytes 528 | tf_op jit(solution)/shard_map/all_gather | solution.py:281
  70.0 4.9 %dynamic-slice_bitcast_fusion.4 = (f32[2,128,1024]{2,1,0:T(8,128)}, f32[2,128,1024]{2,1,0:T(8,128)}, f32[2,128,1024]{2,1,0:T(8,128)}, f32[2,128,1024]{2,1,0:T(8,128)}) fusion(f32[4,2,256,1024]{3,2,1,0:T(8,128)} %param.22, s32[]{:T(128)S(6)} %select_n.318, s32[]{:T(128)S(6)} %select_n.323, s32[]{:T(128)S(6)} %select_n.307, s32[]{:T(128)S(6)} %select_n.312, ...), kind=kLoop, calls=%fused_computation.7 | loop fusion | bytes 8388640 | tf_op jit(solution)/shard_map/dynamic_slice | solution.py:285
  74.9 1.9 collective-permute-start.4
  76.9 4.0 collective-permute-start.5
  80.9 5.8 %collective-permute-start.6 = (f32[2,128,1024]{2,1,0:T(8,128)}, f32[2,128,1024]{2,1,0:T(8,128)S(1)}, u32[]{:S(2)}, u32[]{:S(2)}) collective-permute-start(f32[2,128,1024]{2,1,0:T(8,128)} %get-tuple-element.77), channel_id=1, source_target_pairs={{0,4},{6,5},{4,6},{7,0},{10,7},{9,1},{8,12},{11,2},{14,13},{13,3},... | collective-permute-start | bytes 3145736 | tf_op jit(solution)/shard_map/ppermute | solution.py:300
  86.8 7.5 %dynamic-slice_bitcast_fusion = (f32[2,256,1024]{2,1,0:T(8,128)}, f32[2,256,1024]{2,1,0:T(8,128)}, f32[2,256,1024]{2,1,0:T(8,128)}, f32[2,256,1024]{2,1,0:T(8,128)}) fusion(f32[4,2,256,1024]{3,2,1,0:T(8,128)} %param.22, s32[]{:T(128)S(6)} %select_n.279, s32[]{:T(128)S(6)} %select_n.277, s32[]{:T(128)S(6)} %select_n.275, s32[]{:T(128)S(6)} %select_n.267), kind=kLoop, calls=%fused_computation.2 | loop fusion | bytes 16777232 | tf_op jit(solution)/shard_map/jit(dynamic_index_in_dim)/squeeze | solution.py:289
  94.3 3.4 collective-permute-start
  97.7 4.2 collective-permute-start.1
  101.9 31.2 %collective-permute-done.4.refs_0_ = f32[2,128,1024]{2,1,0:T(8,128)S(1)} collective-permute-done((f32[2,128,1024]{2,1,0:T(8,128)}, f32[2,128,1024]{2,1,0:T(8,128)S(1)}, u32[]{:S(2)}, u32[]{:S(2)}) %collective-permute-start.4) | collective-permute-done | bytes 1048608 | tf_op jit(solution)/shard_map/ppermute | solution.py:300
  133.1 21.8 %collective-permute-start.2 = (f32[2,256,1024]{2,1,0:T(8,128)}, f32[2,256,1024]{2,1,0:T(8,128)}, u32[]{:S(2)}, u32[]{:S(2)}) collective-permute-start(f32[2,256,1024]{2,1,0:T(8,128)} %get-tuple-element.81), channel_id=1, source_target_pairs={{3,0},{0,4},{1,1},{2,5},{7,2},{4,6},{5,3},{6,7},{11,8},{8,12},{9,9... | collective-permute-start | bytes 6291464 | tf_op jit(solution)/shard_map/ppermute | solution.py:291
  154.9 1.9 collective-permute-start.3
  156.8 34.5 %collective-permute-start.7 = (f32[2,128,1024]{2,1,0:T(8,128)}, f32[2,128,1024]{2,1,0:T(8,128)}, u32[]{:S(2)}, u32[]{:S(2)}) collective-permute-start(f32[2,128,1024]{2,1,0:T(8,128)} %get-tuple-element.76), channel_id=1, source_target_pairs={{1,4},{7,5},{5,6},{4,0},{11,7},{10,1},{9,12},{8,2},{15,13},{14,3},... | collective-permute-start | bytes 3145736 | tf_op jit(solution)/shard_map/ppermute | solution.py:300
  208.6 38.0 %collective-permute-done.7.refs_0_ = f32[2,128,1024]{2,1,0:T(8,128)} collective-permute-done((f32[2,128,1024]{2,1,0:T(8,128)}, f32[2,128,1024]{2,1,0:T(8,128)}, u32[]{:S(2)}, u32[]{:S(2)}) %collective-permute-start.7) | collective-permute-done | bytes 1048608 | tf_op jit(solution)/shard_map/ppermute | solution.py:300
  246.7 2.5 shard_map.228
  250.8 68.0 %collective-permute-done.2 = f32[2,256,1024]{2,1,0:T(8,128)} collective-permute-done((f32[2,256,1024]{2,1,0:T(8,128)}, f32[2,256,1024]{2,1,0:T(8,128)}, u32[]{:S(2)}, u32[]{:S(2)}) %collective-permute-start.2) | collective-permute-done | bytes 2097184 | tf_op jit(solution)/shard_map/ppermute | solution.py:291
  318.9 10.5 %dynamic-slice_select_fusion.1 = (f32[2,128,1024]{2,1,0:T(8,128)}, f32[2,128,1024]{2,1,0:T(8,128)}, f32[2,128,1024]{2,1,0:T(8,128)}, f32[2,128,1024]{2,1,0:T(8,1...) fusion(f32[2,256,1024]{2,1,0:T(8,128)} %collective-permute-done, ...), kind=kLoop, calls=%fused_computation.12 | loop fusion | flops 1048576 | bytes 25165836 | tf_op jit(solution)/shard_map/jit(_where)/select_n | solution.py:321
  329.4 3.2 pad_maximum_fusion.1
  332.6 1.9 collective-permute-start.10
  334.6 1.6 pad_maximum_fusion
  336.2 2.1 collective-permute-start.9
  346.0 12.2 %shard_map.229 = f32[128,1024]{1,0:T(8,128)S(1)} custom-call(f32[2,256,512]{2,1,0:T(8,128)S(1)} %get-tuple-element.38.refs_0_, f32[2,256,512]{2,1,0:T(8,128)S(1)} %get-tuple-element.39.refs_1_, f32[2,256,512]{2,1,0:T(8,128)} %copy-done.39, f32[2,256,512]{2,1,0:T(8,128)} %copy-done.40, f32[2,256,512]{2,1,0:T(8,128)} %copy-done.29, f32[2,256,512]{2,1,0:T(8,128)} %copy-done.30, ...), custom_call_target="tpu_custom_call" | custom-call | flops 12000000000 | bytes 36000000 | tf_op jit(solution)/shard_map/pallas_call | solution.py:239
  358.2 38.7 %collective-permute-start.8 = (f32[128,1024]{1,0:T(8,128)S(1)}, f32[128,1024]{1,0:T(8,128)}, u32[]{:S(2)}, u32[]{:S(2)}) collective-permute-start(f32[128,1024]{1,0:T(8,128)S(1)} %shard_map.229), channel_id=1, source_target_pairs={{0,0},{4,1},{1,2},{5,3},{2,4},{6,5},{3,6},{7,7},{8,8},{12,9},{9,10... | collective-permute-start | bytes 1572872 | tf_op jit(solution)/shard_map/ppermute | solution.py:314
  396.8 1.3 shard_map.230
  399.4 1.3 shard_map.232
  400.8 1.3 shard_map.233
  402.1 2.2 fusion.2
  408.9 1.8 fusion.3
  410.7 1.3 shard_map.234
  415.3 12.0 %shard_map.238 = f32[128,1024]{1,0:T(8,128)S(1)} custom-call(f32[2,256,512]{2,1,0:T(8,128)S(1)} %get-tuple-element.54.refs_0_, f32[2,256,512]{2,1,0:T(8,128)S(1)} %get-tuple-element.55.refs_1_, f32[2,256,512]{2,1,0:T(8,128)} %copy-done.33, f32[2,256,512]{2,1,0:T(8,128)} %copy-done.34, f32[2,256,512]{2,1,0:T(8,128)} %copy-done.37, f32[2,256,512]{2,1,0:T(8,128)} %copy-done.35, ...), custom_call_target="tpu_custom_call" | custom-call | flops 12000000000 | bytes 36000000 | tf_op jit(solution)/shard_map/pallas_call | solution.py:239
  427.3 13.6 %collective-permute-start.11 = (f32[128,1024]{1,0:T(8,128)S(1)}, f32[128,1024]{1,0:T(8,128)S(1)}, u32[]{:S(2)}, u32[]{:S(2)}) collective-permute-start(f32[128,1024]{1,0:T(8,128)S(1)} %shard_map.238), channel_id=1, source_target_pairs={{0,0},{4,1},{1,2},{5,3},{2,4},{6,5},{3,6},{7,7},{8,8},{12,9},{9,10... | collective-permute-start | bytes 1572872 | tf_op jit(solution)/shard_map/ppermute | solution.py:314
  440.9 9.5 %collective-permute-done.11 = f32[128,1024]{1,0:T(8,128)S(1)} collective-permute-done((f32[128,1024]{1,0:T(8,128)S(1)}, f32[128,1024]{1,0:T(8,128)S(1)}, u32[]{:S(2)}, u32[]{:S(2)}) %collective-permute-start.11) | collective-permute-done | bytes 524320 | tf_op jit(solution)/shard_map/ppermute | solution.py:314
  451.6 1.6 fusion
  (124 shorter events, 31.5 us)
Async XLA Ops:
  74.9 58.1 %collective-permute-start.4 = (f32[2,128,1024]{2,1,0:T(8,128)}, f32[2,128,1024]{2,1,0:T(8,128)S(1)}, u32[]{:S(2)}, u32[]{:S(2)}) collective-permute-start(f32[2,128,1024]{2,1,0:T(8,128)} %get-tuple-element.79), channel_id=1, source_target_pairs={{2,4},{4,5},{6,6},{5,0},{8,7},{11,1},{10,12},{9,2},{12,13},{15,3},... | collective-permute-start | bytes 3145736 | tf_op jit(solution)/shard_map/ppermute | solution.py:300
  76.9 78.0 %collective-permute-start.5 = (f32[2,128,1024]{2,1,0:T(8,128)}, f32[2,128,1024]{2,1,0:T(8,128)S(1)}, u32[]{:S(2)}, u32[]{:S(2)}) collective-permute-start(f32[2,128,1024]{2,1,0:T(8,128)} %get-tuple-element.78), channel_id=1, source_target_pairs={{3,4},{5,5},{7,6},{6,0},{9,7},{8,1},{11,12},{10,2},{13,13},{12,3},... | collective-permute-start | bytes 3145736 | tf_op jit(solution)/shard_map/ppermute | solution.py:300
  80.9 75.9 %collective-permute-start.6 = (f32[2,128,1024]{2,1,0:T(8,128)}, f32[2,128,1024]{2,1,0:T(8,128)S(1)}, u32[]{:S(2)}, u32[]{:S(2)}) collective-permute-start(f32[2,128,1024]{2,1,0:T(8,128)} %get-tuple-element.77), channel_id=1, source_target_pairs={{0,4},{6,5},{4,6},{7,0},{10,7},{9,1},{8,12},{11,2},{14,13},{13,3},... | collective-permute-start | bytes 3145736 | tf_op jit(solution)/shard_map/ppermute | solution.py:300
  86.8 110.4 %copy-start.10 = (bf16[256,256]{1,0:T(8,128)(2,1)S(1)}, bf16[256,256]{1,0:T(8,128)(2,1)}, u32[]{:S(2)}) copy-start(bf16[256,256]{1,0:T(8,128)(2,1)} %constant.294.clone.refs_7_.refs_16_) | copy-start | bytes 393220
  86.8 110.4 %copy-start.11 = (bf16[256,256]{1,0:T(8,128)(2,1)S(1)}, bf16[256,256]{1,0:T(8,128)(2,1)}, u32[]{:S(2)}) copy-start(bf16[256,256]{1,0:T(8,128)(2,1)} %constant.295.clone.refs_8_.refs_17_) | copy-start | bytes 393220
  86.8 110.4 %copy-start.22 = (bf16[256,256]{1,0:T(8,128)(2,1)S(1)}, bf16[256,256]{1,0:T(8,128)(2,1)}, u32[]{:S(2)}) copy-start(bf16[256,256]{1,0:T(8,128)(2,1)} %constant.288.clone.refs_1_) | copy-start | bytes 393220
  94.3 156.5 %collective-permute-start = (f32[2,256,1024]{2,1,0:T(8,128)}, f32[2,256,1024]{2,1,0:T(8,128)}, u32[]{:S(2)}, u32[]{:S(2)}) collective-permute-start(f32[2,256,1024]{2,1,0:T(8,128)} %get-tuple-element.83), channel_id=1, source_target_pairs={{1,0},{2,4},{3,1},{0,5},{5,2},{6,6},{7,3},{4,7},{9,8},{10,12},{11,... | collective-permute-start | bytes 6291464 | tf_op jit(solution)/shard_map/ppermute | solution.py:291
  97.7 153.2 %collective-permute-start.1 = (f32[2,256,1024]{2,1,0:T(8,128)}, f32[2,256,1024]{2,1,0:T(8,128)}, u32[]{:S(2)}, u32[]{:S(2)}) collective-permute-start(f32[2,256,1024]{2,1,0:T(8,128)} %get-tuple-element.82), channel_id=1, source_target_pairs={{2,0},{3,4},{0,1},{1,5},{6,2},{7,6},{4,3},{5,7},{10,8},{11,12},{8,... | collective-permute-start | bytes 6291464 | tf_op jit(solution)/shard_map/ppermute | solution.py:291
  133.1 185.8 %collective-permute-start.2 = (f32[2,256,1024]{2,1,0:T(8,128)}, f32[2,256,1024]{2,1,0:T(8,128)}, u32[]{:S(2)}, u32[]{:S(2)}) collective-permute-start(f32[2,256,1024]{2,1,0:T(8,128)} %get-tuple-element.81), channel_id=1, source_target_pairs={{3,0},{0,4},{1,1},{2,5},{7,2},{4,6},{5,3},{6,7},{11,8},{8,12},{9,9... | collective-permute-start | bytes 6291464 | tf_op jit(solution)/shard_map/ppermute | solution.py:291
  154.9 164.0 %collective-permute-start.3 = (f32[2,256,1024]{2,1,0:T(8,128)}, f32[2,256,1024]{2,1,0:T(8,128)}, u32[]{:S(2)}, u32[]{:S(2)}) collective-permute-start(f32[2,256,1024]{2,1,0:T(8,128)} %get-tuple-element.80), channel_id=1, source_target_pairs={{0,0},{1,4},{2,1},{3,5},{4,2},{5,6},{6,3},{7,7},{8,8},{9,12},{10,9... | collective-permute-start | bytes 6291464 | tf_op jit(solution)/shard_map/ppermute | solution.py:291
  156.8 89.8 %collective-permute-start.7 = (f32[2,128,1024]{2,1,0:T(8,128)}, f32[2,128,1024]{2,1,0:T(8,128)}, u32[]{:S(2)}, u32[]{:S(2)}) collective-permute-start(f32[2,128,1024]{2,1,0:T(8,128)} %get-tuple-element.76), channel_id=1, source_target_pairs={{1,4},{7,5},{5,6},{4,0},{11,7},{10,1},{9,12},{8,2},{15,13},{14,3},... | collective-permute-start | bytes 3145736 | tf_op jit(solution)/shard_map/ppermute | solution.py:300
  329.4 5.2 %copy-start.49 = (f32[2,128,1024]{2,1,0:T(8,128)S(1)}, f32[2,128,1024]{2,1,0:T(8,128)}, u32[]{:S(2)}) copy-start(f32[2,128,1024]{2,1,0:T(8,128)} %get-tuple-element.115) | copy-start | bytes 3145732
  329.4 5.2 %copy-start.50 = (f32[2,128,1024]{2,1,0:T(8,128)S(1)}, f32[2,128,1024]{2,1,0:T(8,128)}, u32[]{:S(2)}) copy-start(f32[2,128,1024]{2,1,0:T(8,128)} %get-tuple-element.116) | copy-start | bytes 3145732
  332.6 69.5 %collective-permute-start.10 = (f32[4,128,1024]{2,1,0:T(8,128)}, f32[4,128,1024]{2,1,0:T(8,128)}, u32[]{:S(2)}, u32[]{:S(2)}) collective-permute-start(f32[4,128,1024]{2,1,0:T(8,128)} %pad_maximum_fusion.1), channel_id=1, source_target_pairs={{4,0},{5,1},{6,2},{8,4},{12,8},{9,5},{13,9},{10,6},{14,10},{11,7},... | collective-permute-start | bytes 6291464 | tf_op jit(solution)/shard_map/ppermute | solution.py:325
  334.6 3.8 copy-start.3
  334.6 3.8 copy-start.7
  334.6 3.8 copy-start.9
  334.6 3.8 copy-start.24
  334.6 3.8 copy-start.26
  334.6 3.8 copy-start.28
  336.2 72.7 %collective-permute-start.9 = (f32[4,128,1024]{2,1,0:T(8,128)}, f32[4,128,1024]{2,1,0:T(8,128)}, u32[]{:S(2)}, u32[]{:S(2)}) collective-permute-start(f32[4,128,1024]{2,1,0:T(8,128)} %pad_maximum_fusion), channel_id=1, source_target_pairs={{4,0},{5,1},{6,2},{8,4},{12,8},{9,5},{13,9},{10,6},{14,10},{11,7},... | collective-permute-start | bytes 6291464 | tf_op jit(solution)/shard_map/ppermute | solution.py:325
  343.3 2.5 copy-start.4
  343.4 2.5 copy-start.5
  343.4 2.5 copy-start.12
  343.4 2.5 copy-start.13
  343.4 2.5 copy-start.14
  343.4 2.5 copy-start.15
  343.4 2.5 copy-start.16
  343.4 2.5 copy-start.17
  343.4 2.5 copy-start.18
  358.2 82.7 %collective-permute-start.8 = (f32[128,1024]{1,0:T(8,128)S(1)}, f32[128,1024]{1,0:T(8,128)}, u32[]{:S(2)}, u32[]{:S(2)}) collective-permute-start(f32[128,1024]{1,0:T(8,128)S(1)} %shard_map.229), channel_id=1, source_target_pairs={{0,0},{4,1},{1,2},{5,3},{2,4},{6,5},{3,6},{7,7},{8,8},{12,9},{9,10... | collective-permute-start | bytes 1572872 | tf_op jit(solution)/shard_map/ppermute | solution.py:314
  427.3 23.1 %collective-permute-start.11 = (f32[128,1024]{1,0:T(8,128)S(1)}, f32[128,1024]{1,0:T(8,128)S(1)}, u32[]{:S(2)}, u32[]{:S(2)}) collective-permute-start(f32[128,1024]{1,0:T(8,128)S(1)} %shard_map.238), channel_id=1, source_target_pairs={{0,0},{4,1},{1,2},{5,3},{2,4},{6,5},{3,6},{7,7},{8,8},{12,9},{9,10... | collective-permute-start | bytes 1572872 | tf_op jit(solution)/shard_map/ppermute | solution.py:314
  (31 other events, 44.5 us)

commit v3 on v2

--- a/solution.py
+++ b/solution.py
@@ -1,4 +1,3 @@
-import functools
 import math
 
 import jax
@@ -113,17 +112,20 @@
     return re * gain, im * gain
 
 
+def times(a, b):
+    return a[0] * b[0] - a[1] * b[1], a[1] * b[0] + a[0] * b[1]
+
+
 def lane_is(shape, lane):
     return lax.broadcasted_iota(jnp.int32, shape, 1) == lane
 
 
-def spectrum_kernel(slot, count, *refs):
-    strips, (f0h, f0l, f2h, f2l, f1h, f1l, rh, rl) = refs[:count], refs[count : count + 8]
-    spec, column = refs[count + 8 :]
-    depth, across, along = strips[0].shape
+def spectrum_kernel(strip, f0h, f0l, f2h, f2l, f1h, f1l, rh, rl, spec, column):
+    depth, across, along = strip.shape
     q = along // 4
     h = q // 2
-    x = sum(strip[...] for strip in strips).reshape(depth * across, along)
+    part = pl.program_id(0)
+    x = strip[...].reshape(depth * across, along)
     x0, x1, x2, x3 = (x[:, n * q : (n + 1) * q] for n in range(4))
     s02, s13 = x0 + x2, x1 + x3
     out0 = by_right(s02 + s13, f0h, f0l)
@@ -133,23 +135,20 @@
     first = lane_is(imag0.shape, 0)
     real = jnp.concatenate((out0[:, :h], out2[:, :h], out1[:, :q]), axis=1)
     imag = jnp.concatenate((jnp.where(first, 0.0, imag0), out2[:, h:], out1[:, q:]), axis=1)
-    middles = jnp.zeros(column.shape, F32)
+    middles = jnp.where(part == 0, 0.0, column[...])
     for n in range(depth):
         rows = slice(n * across, (n + 1) * across)
         spec[n] = by_left(rh, rl, jnp.concatenate((real[rows], imag[rows]), axis=0))
         middle = jnp.broadcast_to(imag0[rows, 0:1], column.shape)
-        middles = jnp.where(lane_is(column.shape, slot * depth + n), middle, middles)
+        middles = jnp.where(lane_is(column.shape, part * depth + n), middle, middles)
     column[...] = middles
 
 
-def pair_kernel(parts, *refs):
-    own, other = refs[:parts], refs[parts : 2 * parts]
-    own_cols, other_cols = refs[2 * parts : 3 * parts], refs[3 * parts : 4 * parts]
-    (ah, al, zh, zl), back = refs[4 * parts : 4 * parts + 4], refs[4 * parts + 4 : 4 * parts + 14]
-    surface, spec, column = refs[4 * parts + 14 :]
+def pair_kernel(turn, own, other, own_col, other_col, turn_row, *refs):
+    (ah, al, zh, zl), back = refs[:4], refs[4:14]
+    surface, spec, column = refs[14:]
     b0h, b0l, b2h, b2l, b1h, b1l, rh, rl, bzh, bzl = back
-    per = own[0].shape[0]
-    depth = per * parts
+    depth = own.shape[0]
     across, along = surface.shape
     q = along // 4
     h = q // 2
@@ -159,11 +158,12 @@
         im_rows = pl.ds(pl.multiple_of(across + 8 * i, 8), 8)
         for lane in range(0, along // 2, LANES):
             lanes = slice(lane, lane + LANES)
-            load = lambda group: [
-                (group[z // per][z % per, re_rows, lanes], group[z // per][z % per, im_rows, lanes])
-                for z in range(depth)
+            load = lambda held: [(held[z, re_rows, lanes], held[z, im_rows, lanes]) for z in range(depth)]
+            theirs = [
+                times(point, (turn[0, u], turn[1, u]))
+                for u, point in enumerate(fft(load(other), -1))
             ]
-            white = [whiten(a, b) for a, b in zip(fft(load(own), -1), fft(load(other), -1))]
+            white = [whiten(a, b) for a, b in zip(fft(load(own), -1), theirs)]
             for z, (re, im) in enumerate(fft(white, 1)):
                 spec[z, re_rows, lanes] = re
                 spec[z, im_rows, lanes] = im
@@ -171,12 +171,13 @@
 
     lax.fori_loop(0, across // 8, meet, 0)
 
-    def edge(group):
-        turned = by_left(ah.at[:, :across], al.at[:, :across], sum(c[...] for c in group))
+    def edge(held):
+        turned = by_left(ah.at[:, :across], al.at[:, :across], held[...])
         turned = by_right(jnp.concatenate((turned[:across], turned[across:]), axis=1), zh, zl)
         return turned[:, :LANES], turned[:, LANES:]
 
-    white = whiten(edge(own_cols), edge(other_cols))
+    theirs = times(edge(other_col), (turn_row[0:1, :], turn_row[1:2, :]))
+    white = whiten(edge(own_col), theirs)
     back_z = by_right(jnp.concatenate(white, axis=1), bzh, bzl)
     back_z = jnp.concatenate((back_z[:, :LANES], back_z[:, LANES:]), axis=0)
     column[...] = by_left(rh.at[:across], rl.at[:across], back_z)
@@ -213,43 +214,51 @@
 PARAMS = pltpu.CompilerParams(vmem_limit_bytes=48 * 1024 * 1024)
 
 
-def spectrum_of(strips, slot, forth):
-    depth, across, along = strips[0].shape
+def whole(shape):
+    return pl.BlockSpec(shape, lambda i: (0,) * len(shape))
+
+
+def spectrum_of(strip, per, forth):
+    depth, across, along = strip.shape
     return pl.pallas_call(
-        functools.partial(spectrum_kernel, slot, len(strips)),
+        spectrum_kernel,
+        grid=(depth // per,),
         out_shape=(
             jax.ShapeDtypeStruct((depth, 2 * across, along // 2), F32),
             jax.ShapeDtypeStruct((across, LANES), F32),
         ),
-        in_specs=[VMEM] * (len(strips) + 8),
-        out_specs=(VMEM, VMEM),
+        in_specs=[pl.BlockSpec((per, across, along), lambda i: (i, 0, 0))]
+        + [whole(table.shape) for table in forth[:8]],
+        out_specs=(
+            pl.BlockSpec((per, 2 * across, along // 2), lambda i: (i, 0, 0)),
+            whole((across, LANES)),
+        ),
         compiler_params=PARAMS,
         cost_estimate=pl.CostEstimate(
-            flops=2 * 10**9, bytes_accessed=16 * 10**6, transcendentals=0
+            flops=6 * 10**9, bytes_accessed=10 * 10**6, transcendentals=0
         ),
-    )(*strips, *forth[:8])
-
-
-def pair_of(own, other, forth, back):
-    parts = len(own)
-    per, rows, half = own[0][0].shape
+    )(strip, *forth[:8])
+
+
+def pair_of(turn, own, other, forth, back):
+    depth, rows, half = own[0].shape
     across, along = rows // 2, 2 * half
-    operands = [x[0] for x in own] + [x[0] for x in other] + [x[1] for x in own] + [x[1] for x in other]
-    operands += forth[6:10] + back
+    row = jnp.pad(turn, ((0, 0), (0, LANES - depth)))
+    operands = [own[0], other[0], own[1], other[1], row] + forth[6:10] + back
     return pl.pallas_call(
-        functools.partial(pair_kernel, parts),
+        pair_kernel,
         out_shape=jax.ShapeDtypeStruct((across, along), F32),
-        in_specs=[VMEM] * len(operands),
+        in_specs=[pl.BlockSpec(memory_space=pltpu.SMEM)] + [VMEM] * len(operands),
         out_specs=VMEM,
         scratch_shapes=[
-            pltpu.VMEM((parts * per, rows, half), F32),
+            pltpu.VMEM((depth, rows, half), F32),
             pltpu.VMEM((across, LANES), F32),
         ],
         compiler_params=PARAMS,
         cost_estimate=pl.CostEstimate(
             flops=12 * 10**9, bytes_accessed=36 * 10**6, transcendentals=0
         ),
-    )(*operands)
+    )(turn, *operands)
 
 
 def on_device(stored, offsets):
@@ -258,7 +267,8 @@
     count = lax.axis_size(axes)
     group = PER_CHIP * slabs
     per, along = stored.shape[1], stored.shape[3]
-    forth, back = make_tables(per * slabs, A, along)
+    depth = per * slabs
+    forth, back = make_tables(depth, A, along)
     strides = (1, GC)
 
     def place_of(t):
@@ -269,64 +279,43 @@
         to = t - strides[rnd]
         return to >= 0 and (rnd == 1 or to % GC != GC - 1)
 
-    def holder(t, step, of):
-        return t // slabs * slabs + (of - step) % slabs
+    def holder(t, step):
+        return t // slabs * slabs + (t - step) % slabs
 
     near = [(t, t - strides[1 - t % 2]) for t in range(count) if gives(1 - t % 2, t)]
     far = [(t, t - strides[t % 2]) for t in range(count) if gives(t % 2, t)]
 
     tile, slab = lax.axis_index("tile"), lax.axis_index("slab")
-    here = tile // PER_CHIP * group + slab * PER_CHIP + tile % PER_CHIP
-    odd = here % 2
-    table = lax.all_gather(offsets[:, :, 0], axes)
-    stored, table = lax.optimization_barrier((stored, table))
-
-    def cut(planes, at):
-        return lax.dynamic_slice_in_dim(planes, at, A, 1)
-
-    bands, fars = [], []
+    odd = tile % PER_CHIP
+    mine = lax.ppermute(offsets[:, :, 0], axes, [(t, place_of(t)) for t in range(count)])
+    bands = []
     for step in range(slabs):
         planes = lax.dynamic_index_in_dim(stored, (slab + step) % slabs, 0, False)
-        bands.append(
-            lax.ppermute(planes, axes, [(holder(t, step, t), place_of(t)) for t in range(count)])
+        pairs = [(holder(t, step), place_of(t)) for t in range(count)]
+        bands.append(lax.ppermute(planes, axes, pairs))
+
+    def cut(rnd, which):
+        return jnp.concatenate(
+            [lax.dynamic_slice_in_dim(band, mine[rnd, which], A, 1) for band in bands[::-1]]
         )
-        ahead = (slab + step) % slabs
-        which = jnp.where(
-            (ahead + strides[0]) % 2 == 0, (ahead + strides[0]) % slabs, (ahead + strides[1]) % slabs
-        )
-        planes = lax.dynamic_index_in_dim(stored, which, 0, False)
-        at = table[tile * slabs + which, which % 2, 1]
-        fars.append(
-            lax.ppermute(
-                cut(planes, at), axes, [(holder(t, step, to), place_of(to)) for t, to in far]
-            )
-        )
-
-    def spectra(pieces):
-        return [spectrum_of([piece], n, forth) for n, piece in enumerate(pieces[::-1])]
-
-    def own(rnd):
-        at = table[here, rnd, 0]
-        return spectra([cut(band, at) for band in bands])
-
-    def surface_of(rnd, arrived):
-        surface = pair_of(own(rnd), spectra(arrived), forth, back)
+
+    def arrive(strip, pairs):
+        return lax.ppermute(strip, axes, [(place_of(t), place_of(to)) for t, to in pairs])
+
+    angles = [phases(np.arange(depth), [per * stride], depth) for stride in strides]
+    turns = jnp.asarray(np.stack([[c[:, 0], -s[:, 0]] for c, s in angles]), F32)
+
+    def surface_of(rnd, strip):
+        own = spectrum_of(cut(rnd, 0), per, forth)
+        turn = lax.dynamic_index_in_dim(turns, rnd, 0, False)
+        surface = pair_of(turn, own, spectrum_of(strip, per, forth), forth, back)
         return lax.ppermute(surface, axes, [(place_of(t), t) for t in range(count)])
 
-    given = [cut(band, table[here, 1 - odd, 1]) for band in bands]
-    nears = [None] * slabs
-    for first in (1, 0):
-        steps = range(first, slabs, 2)
-        ready = [
-            jnp.where(odd == 1, given[(s + strides[0]) % slabs], given[(s + strides[1]) % slabs])
-            for s in steps
-        ]
-        pairs = [(place_of(t), place_of(to)) for t, to in near]
-        arrived = lax.ppermute(jnp.concatenate(ready), axes, pairs)
-        for n, s in enumerate(steps):
-            nears[s] = arrived[n * per : (n + 1) * per]
-    from_far = surface_of(1 - odd, fars)
-    from_near = surface_of(odd, nears)
+    given_far, given_near = cut(odd, 1), cut(1 - odd, 1)
+    strip_near = arrive(given_near, near)
+    strip_far = arrive(given_far, far)
+    from_near = surface_of(odd, strip_near)
+    from_far = surface_of(1 - odd, strip_far)
     home_odd = (tile * slabs + slab) % 2 == 1
     surface = jnp.stack(
         (jnp.where(home_odd, from_far, from_near), jnp.where(home_odd, from_near, from_far))

time: 455 us -> 392 us (0.86)
  blocking collectives: 60.5 us -> 0 us
  waiting for transfers between devices: 147 us -> 168 us
  other arithmetic: 18.1 us -> 8.1 us
  between operations: 15.2 us -> 8.76 us
  local copies, waits for them, and re-layouts: 32.4 us -> 26.3 us
  starting transfers between devices: 134 us -> 128 us
  Pallas kernels: 46.3 us -> 51.5 us
    all_gather x1 -> x0, blocking collectives: 60.5 us -> none  [on_device(): table = lax.all_gather(offsets[:, :, 0], axes)]
    ppermute x2, starting transfers between devices: 52.2 us -> 7.12 us  [surface_of(): return lax.ppermute(surface, axes, [(place_of(t), t) for t in range(count)])]
    ppermute x10 -> x7, starting transfers between devices: 81.6 us -> 120 us  [the longest x2 95.4 us: arrive(): lax.ppermute(strip, axes, [(place_of(t), place_of(to)) for t, to in pairs])]
    ppermute x10 -> x7, waiting for transfers between devices: 137 us -> 154 us  [the longest x1 113 us: on_device(): lax.ppermute(offsets[:, :, 0], axes, [(t, place_of(t)) for t in range(cou...]
    select_n x1 -> x0, other arithmetic: 10.5 us -> none  [on_device(): jnp.where(odd == 1, given[(s + strides[0]) % slabs], given[(s + strides[1...]
    unnamed x102 -> x52, local copies, waits for them, and re-layouts: 15 us -> 8 us
    pallas_call x18 -> x6, Pallas kernels: 46.3 us -> 51.5 us  [the longest x4 25.8 us: spectrum_of(): pl.pallas_call(spectrum_kernel, grid=(depth // per,), out_shape=(jax.Shap...]
    dynamic_slice x2 -> x5, local copies, waits for them, and re-layouts: 5.61 us -> 10.7 us  [the longest x4 10.1 us: cut(): lax.dynamic_slice_in_dim(band, mine[rnd, which], A, 1)]
  transfers between devices with their start and end apart: 12 -> 9, of which waited for: 4 -> 4; matrix products, arithmetic and copies ran while one was open for 3% -> 4% of each run, Pallas kernels for 10% -> 13%
where the time goes in v3:
time: 392 us; the launch traced here: 390 us
  waiting for transfers between devices  168 us (43%)
  starting transfers between devices  128 us (33%)
  Pallas kernels  51.5 us (13%)
  local copies, waits for them, and re-layouts  26.3 us (7%)
  between operations  8.76 us (2%)
  other arithmetic  8.1 us (2%)
    ppermute x1, waiting for transfers between devices, on_device(): lax.ppermute(offsets[:, :, 0], axes, [(t, place_of(t)) for t in range(cou...  113 us
    ppermute x2, starting transfers between devices, arrive(): lax.ppermute(strip, axes, [(place_of(t), place_of(to)) for t, to in pairs])  95.4 us
    ppermute x2, waiting for transfers between devices, arrive(): lax.ppermute(strip, axes, [(place_of(t), place_of(to)) for t, to in pairs])  40.8 us
    pallas_call x4, Pallas kernels, spectrum_of(): pl.pallas_call(spectrum_kernel, grid=(depth // per,), out_shape=(jax.Shap...  25.8 us
    pallas_call x2, Pallas kernels, pair_of(): pl.pallas_call(pair_kernel, out_shape=jax.ShapeDtypeStruct((across, along...  25.7 us
    ppermute x4, starting transfers between devices, on_device(): bands.append(lax.ppermute(planes, axes, pairs))  21.4 us
    ppermute x2, waiting for transfers between devices, surface_of(): return lax.ppermute(surface, axes, [(place_of(t), t) for t in range(count)])  14 us
    dynamic_slice x4, local copies, waits for them, and re-layouts, cut(): lax.dynamic_slice_in_dim(band, mine[rnd, which], A, 1)  10.1 us
  transfers between devices with their start and end apart: 9, of which 4 were waited for; matrix products, arithmetic and copies ran while one was open for 4% of the time, Pallas kernels for 13%

profile of v3, /device:TPU:28, one launch (start us, length us, event | category | flops | bytes accessed | tf_op | source)
XLA Modules:
  0.0 390.0 jit_solution(8363547564014123482)
XLA Ops:
  0.7 7.5 %dynamic-slice_bitcast_fusion.3 = (f32[2,256,1024]{2,1,0:T(8,128)}, f32[2,256,1024]{2,1,0:T(8,128)}, f32[2,256,1024]{2,1,0:T(8,128)}, f32[2,256,1024]{2,1,0:T(8,128)}) fusion(f32[4,2,256,1024]{3,2,1,0:T(8,128)} %param.23, s32[]{:T(128)S(6)} %select_n.104, s32[]{:T(128)S(6)} %select_n.107, s32[]{:T(128)S(6)} %select_n.111, s32[]{:T(128)S(6)} %select_n.109), kind=kLoop, calls=%fused_computation.7 | loop fusion | bytes 16777232 | tf_op jit(solution)/shard_map/jit(dynamic_index_in_dim)/squeeze | solution.py:293
  8.2 1.9 collective-permute-start.4
  10.2 17.4 %collective-permute-start.3 = (f32[2,256,1024]{2,1,0:T(8,128)}, f32[2,256,1024]{2,1,0:T(8,128)}, u32[]{:S(2)}, u32[]{:S(2)}) collective-permute-start(f32[2,256,1024]{2,1,0:T(8,128)} %get-tuple-element.23), channel_id=1, source_target_pairs={{3,0},{0,4},{1,1},{2,5},{7,2},{4,6},{5,3},{6,7},{11,8},{8,12},{9,9... | collective-permute-start | bytes 6291464 | tf_op jit(solution)/shard_map/ppermute | solution.py:295
  27.6 2.0 collective-permute-start
  29.6 3.7 collective-permute-start.1
  33.4 113.0 %collective-permute-done.1 = s32[2,2]{1,0:T(2,128)S(1)} collective-permute-done((s32[2,2]{1,0:T(2,128)S(1)}, s32[2,2]{1,0:T(2,128)S(1)}, u32[]{:S(2)}, u32[]{:S(2)}) %collective-permute-start.1) | collective-permute-done | bytes 48 | tf_op jit(solution)/shard_map/ppermute | solution.py:290
  146.4 0.6 constant_dynamic-slice_fusion.21
  154.5 3.1 constant_dynamic-slice_fusion.10
  157.6 3.2 constant_dynamic-slice_fusion.11
  160.8 3.1 constant_dynamic-slice_fusion.12
  163.9 0.8 constant_dynamic-slice_fusion.13
  164.7 0.3 pad_maximum_fusion.1
  165.0 93.4 %collective-permute-start.5 = (f32[8,128,1024]{2,1,0:T(8,128)S(1)}, f32[8,128,1024]{2,1,0:T(8,128)}, u32[]{:S(2)}, u32[]{:S(2)}) collective-permute-start(f32[8,128,1024]{2,1,0:T(8,128)S(1)} %pad_maximum_fusion.1), channel_id=1, source_target_pairs={{1,4},{2,5},{3,6},{7,0},{8,7},{12,1},{9,12},{13,2},{10,13},{14,3},... | collective-permute-start | bytes 12582920 | tf_op jit(solution)/shard_map/ppermute | solution.py:303
  258.5 2.5 pad_maximum_fusion.3
  260.9 1.9 collective-permute-start.7
  263.0 3.6 pad_maximum_fusion
  266.7 6.5 %shard_map.230 = (f32[8,256,512]{2,1,0:T(8,128)S(1)}, f32[128,128]{1,0:T(8,128)S(1)}) custom-call(f32[8,128,1024]{2,1,0:T(8,128)} %get-tuple-element.50.strip, bf16[256,256]{1,0:T(8,128)(2,1)S(1)} %copy-done.16, bf16[256,256]{1,0:T(8,128)(2,1)S(1)} %copy-done.17, bf16[256,256]{1,0:T(8,128)(2,1)S(1)} %copy-done.18, bf16[256,256]{1,0:T(8,128)(2,1)S(1)} %copy-done.19, ...), custom_call_target="tpu_custom_call" | custom-call | flops 6000000000 | bytes 10000000 | tf_op jit(solution)/shard_map/pallas_call | solution.py:223
  273.2 2.0 copy-done.22
  275.1 6.5 %shard_map.233 = (f32[8,256,512]{2,1,0:T(8,128)S(1)}, f32[128,128]{1,0:T(8,128)S(1)}) custom-call(f32[8,128,1024]{2,1,0:T(8,128)} %get-tuple-element.51.strip, bf16[256,256]{1,0:T(8,128)(2,1)S(1)} %copy-done.16, bf16[256,256]{1,0:T(8,128)(2,1)S(1)} %copy-done.17, bf16[256,256]{1,0:T(8,128)(2,1)S(1)} %copy-done.18, bf16[256,256]{1,0:T(8,128)(2,1)S(1)} %copy-done.19, ...), custom_call_target="tpu_custom_call" | custom-call | flops 6000000000 | bytes 10000000 | tf_op jit(solution)/shard_map/pallas_call | solution.py:223
  281.6 1.9 copy-done.20
  283.6 22.3 %collective-permute-done.5.strip = f32[8,128,1024]{2,1,0:T(8,128)} collective-permute-done((f32[8,128,1024]{2,1,0:T(8,128)S(1)}, f32[8,128,1024]{2,1,0:T(8,128)}, u32[]{:S(2)}, u32[]{:S(2)}) %collective-permute-start.5) | collective-permute-done | bytes 4194336 | tf_op jit(solution)/shard_map/ppermute | solution.py:303
  305.9 6.5 %shard_map.231 = (f32[8,256,512]{2,1,0:T(8,128)S(1)}, f32[128,128]{1,0:T(8,128)S(1)}) custom-call(f32[8,128,1024]{2,1,0:T(8,128)} %collective-permute-done.5.strip, bf16[256,256]{1,0:T(8,128)(2,1)S(1)} %copy-done.16, bf16[256,256]{1,0:T(8,128)(2,1)S(1)} %copy-done.17, bf16[256,256]{1,0:T(8,128)(2,1)S(1)} %copy-done.18, bf16[256,256]{1,0:T(8,128)(2,1)S(1)} %copy-done.19, ...), custom_call_target="tpu_custom_call" | custom-call | flops 6000000000 | bytes 10000000 | tf_op jit(solution)/shard_map/pallas_call | solution.py:223
  312.4 2.0 copy-done.23
  314.5 12.9 %shard_map.232 = f32[128,1024]{1,0:T(8,128)S(1)} custom-call(f32[2,8]{1,0:T(2,128)S(1)} %get-tuple-element.44.turn, f32[8,256,512]{2,1,0:T(8,128)} %copy-done.22, f32[8,256,512]{2,1,0:T(8,128)} %copy-done.23, f32[128,128]{1,0:T(8,128)S(1)} %get-tuple-element.12.own_col, f32[128,128]{1,0:T(8,128)S(1)} %get-tuple-element.13.other_col, ...), custom_call_target="tpu_custom_call" | custom-call | flops 12000000000 | bytes 36000000 | tf_op jit(solution)/shard_map/pallas_call | solution.py:248
  327.3 2.7 collective-permute-start.6
  330.1 18.6 %collective-permute-done.7.strip = f32[8,128,1024]{2,1,0:T(8,128)} collective-permute-done((f32[8,128,1024]{2,1,0:T(8,128)}, f32[8,128,1024]{2,1,0:T(8,128)}, u32[]{:S(2)}, u32[]{:S(2)}) %collective-permute-start.7) | collective-permute-done | bytes 4194336 | tf_op jit(solution)/shard_map/ppermute | solution.py:303
  348.7 6.5 %shard_map.234 = (f32[8,256,512]{2,1,0:T(8,128)S(1)}, f32[128,128]{1,0:T(8,128)S(1)}) custom-call(f32[8,128,1024]{2,1,0:T(8,128)} %collective-permute-done.7.strip, bf16[256,256]{1,0:T(8,128)(2,1)S(1)} %copy-done.16, bf16[256,256]{1,0:T(8,128)(2,1)S(1)} %copy-done.17, bf16[256,256]{1,0:T(8,128)(2,1)S(1)} %copy-done.18, bf16[256,256]{1,0:T(8,128)(2,1)S(1)} %copy-done.19, ...), custom_call_target="tpu_custom_call" | custom-call | flops 6000000000 | bytes 10000000 | tf_op jit(solution)/shard_map/pallas_call | solution.py:223
  355.1 1.9 copy-done.21
  357.1 12.8 %shard_map.235 = f32[128,1024]{1,0:T(8,128)S(1)} custom-call(f32[2,8]{1,0:T(2,128)S(1)} %get-tuple-element.45.turn, f32[8,256,512]{2,1,0:T(8,128)} %copy-done.20, f32[8,256,512]{2,1,0:T(8,128)} %copy-done.21, f32[128,128]{1,0:T(8,128)S(1)} %get-tuple-element.16.own_col, f32[128,128]{1,0:T(8,128)S(1)} %get-tuple-element.17.other_col, ...), custom_call_target="tpu_custom_call" | custom-call | flops 12000000000 | bytes 36000000 | tf_op jit(solution)/shard_map/pallas_call | solution.py:248
  369.9 4.4 %collective-permute-start.8 = (f32[128,1024]{1,0:T(8,128)S(1)}, f32[128,1024]{1,0:T(8,128)S(1)}, u32[]{:S(2)}, u32[]{:S(2)}) collective-permute-start(f32[128,1024]{1,0:T(8,128)S(1)} %shard_map.235), channel_id=1, source_target_pairs={{0,0},{4,1},{1,2},{5,3},{2,4},{6,5},{3,6},{7,7},{8,8},{12,9},{9,10... | collective-permute-start | bytes 1572872 | tf_op jit(solution)/shard_map/ppermute | solution.py:312
  374.3 14.0 %collective-permute-done.8 = f32[128,1024]{1,0:T(8,128)S(1)} collective-permute-done((f32[128,1024]{1,0:T(8,128)S(1)}, f32[128,1024]{1,0:T(8,128)S(1)}, u32[]{:S(2)}, u32[]{:S(2)}) %collective-permute-start.8) | collective-permute-done | bytes 524320 | tf_op jit(solution)/shard_map/ppermute | solution.py:312
  388.4 1.6 fusion
  (58 shorter events, 0.3 us)
Async XLA Ops:
  0.7 28.9 %copy-start.25 = (s32[2,2,1]{1,2,0:T(1,128)S(1)}, s32[2,2,1]{1,2,0:T(1,128)}, u32[]{:S(2)}) copy-start(s32[2,2,1]{1,2,0:T(1,128)} %param.24) | copy-start | bytes 52
  8.2 146.3 %collective-permute-start.4 = (f32[2,256,1024]{2,1,0:T(8,128)}, f32[2,256,1024]{2,1,0:T(8,128)}, u32[]{:S(2)}, u32[]{:S(2)}) collective-permute-start(f32[2,256,1024]{2,1,0:T(8,128)} %get-tuple-element.22), channel_id=1, source_target_pairs={{0,0},{1,4},{2,1},{3,5},{4,2},{5,6},{6,3},{7,7},{8,8},{9,12},{10,9... | collective-permute-start | bytes 6291464 | tf_op jit(solution)/shard_map/ppermute | solution.py:295
  10.2 147.5 %collective-permute-start.3 = (f32[2,256,1024]{2,1,0:T(8,128)}, f32[2,256,1024]{2,1,0:T(8,128)}, u32[]{:S(2)}, u32[]{:S(2)}) collective-permute-start(f32[2,256,1024]{2,1,0:T(8,128)} %get-tuple-element.23), channel_id=1, source_target_pairs={{3,0},{0,4},{1,1},{2,5},{7,2},{4,6},{5,3},{6,7},{11,8},{8,12},{9,9... | collective-permute-start | bytes 6291464 | tf_op jit(solution)/shard_map/ppermute | solution.py:295
  27.6 133.3 %collective-permute-start.2 = (f32[2,256,1024]{2,1,0:T(8,128)}, f32[2,256,1024]{2,1,0:T(8,128)}, u32[]{:S(2)}, u32[]{:S(2)}) collective-permute-start(f32[2,256,1024]{2,1,0:T(8,128)} %get-tuple-element.21), channel_id=1, source_target_pairs={{2,0},{3,4},{0,1},{1,5},{6,2},{7,6},{4,3},{5,7},{10,8},{11,12},{8,... | collective-permute-start | bytes 6291464 | tf_op jit(solution)/shard_map/ppermute | solution.py:295
  27.6 136.3 %collective-permute-start = (f32[2,256,1024]{2,1,0:T(8,128)}, f32[2,256,1024]{2,1,0:T(8,128)S(1)}, u32[]{:S(2)}, u32[]{:S(2)}) collective-permute-start(f32[2,256,1024]{2,1,0:T(8,128)} %get-tuple-element.20), channel_id=1, source_target_pairs={{1,0},{2,4},{3,1},{0,5},{5,2},{6,6},{7,3},{4,7},{9,8},{10,12},{11,... | collective-permute-start | bytes 6291464 | tf_op jit(solution)/shard_map/ppermute | solution.py:295
  29.6 116.8 %collective-permute-start.1 = (s32[2,2]{1,0:T(2,128)S(1)}, s32[2,2]{1,0:T(2,128)S(1)}, u32[]{:S(2)}, u32[]{:S(2)}) collective-permute-start(s32[2,2]{1,0:T(2,128)S(1)} %bitcast.27), channel_id=1, source_target_pairs={{0,0},{1,4},{2,1},{3,5},{4,2},{5,6},{6,3},{7,7},{8,8},{9,12},{10,9... | collective-permute-start | bytes 56 | tf_op jit(solution)/shard_map/ppermute | solution.py:290
  165.0 140.9 %collective-permute-start.5 = (f32[8,128,1024]{2,1,0:T(8,128)S(1)}, f32[8,128,1024]{2,1,0:T(8,128)}, u32[]{:S(2)}, u32[]{:S(2)}) collective-permute-start(f32[8,128,1024]{2,1,0:T(8,128)S(1)} %pad_maximum_fusion.1), channel_id=1, source_target_pairs={{1,4},{2,5},{3,6},{7,0},{8,7},{12,1},{9,12},{13,2},{10,13},{14,3},... | collective-permute-start | bytes 12582920 | tf_op jit(solution)/shard_map/ppermute | solution.py:303
  258.4 4.4 %copy-start.24 = (f32[2,2,8]{2,1,0:T(2,128)S(1)}, f32[2,2,8]{2,1,0:T(2,128)}, u32[]{:S(2)}) copy-start(f32[2,2,8]{2,1,0:T(2,128)} %constant.136.clone) | copy-start | bytes 388
  260.9 87.7 %collective-permute-start.7 = (f32[8,128,1024]{2,1,0:T(8,128)}, f32[8,128,1024]{2,1,0:T(8,128)}, u32[]{:S(2)}, u32[]{:S(2)}) collective-permute-start(f32[8,128,1024]{2,1,0:T(8,128)} %pad_maximum_fusion.3), channel_id=1, source_target_pairs={{4,0},{5,1},{6,2},{8,4},{12,8},{9,5},{13,9},{10,6},{14,10},{11,7},... | collective-permute-start | bytes 12582920 | tf_op jit(solution)/shard_map/ppermute | solution.py:303
  262.9 3.7 copy-start.2
  262.9 3.7 copy-start.3
  262.9 3.7 copy-start.4
  262.9 3.7 copy-start.5
  263.0 3.7 copy-start.16
  263.0 3.7 copy-start.17
  263.0 3.7 copy-start.18
  263.0 3.7 copy-start.19
  283.5 30.9 %copy-start = (bf16[512,512]{1,0:T(8,128)(2,1)S(1)}, bf16[512,512]{1,0:T(8,128)(2,1)}, u32[]{:S(2)}) copy-start(bf16[512,512]{1,0:T(8,128)(2,1)} %constant.130.clone.refs_8_) | copy-start | bytes 1572868
  283.5 30.9 %copy-start.1 = (bf16[512,512]{1,0:T(8,128)(2,1)S(1)}, bf16[512,512]{1,0:T(8,128)(2,1)}, u32[]{:S(2)}) copy-start(bf16[512,512]{1,0:T(8,128)(2,1)} %constant.131.clone.refs_9_) | copy-start | bytes 1572868
  283.5 30.9 %copy-start.6 = (bf16[256,256]{1,0:T(8,128)(2,1)S(1)}, bf16[256,256]{1,0:T(8,128)(2,1)}, u32[]{:S(2)}) copy-start(bf16[256,256]{1,0:T(8,128)(2,1)} %constant.124.clone.refs_2_) | copy-start | bytes 393220
  283.5 30.9 %copy-start.7 = (bf16[256,256]{1,0:T(8,128)(2,1)S(1)}, bf16[256,256]{1,0:T(8,128)(2,1)}, u32[]{:S(2)}) copy-start(bf16[256,256]{1,0:T(8,128)(2,1)} %constant.125.clone.refs_3_) | copy-start | bytes 393220
  283.5 30.9 %copy-start.8 = (bf16[256,256]{1,0:T(8,128)(2,1)S(1)}, bf16[256,256]{1,0:T(8,128)(2,1)}, u32[]{:S(2)}) copy-start(bf16[256,256]{1,0:T(8,128)(2,1)} %constant.126.clone.refs_4_) | copy-start | bytes 393220
  283.5 30.9 %copy-start.9 = (bf16[256,256]{1,0:T(8,128)(2,1)S(1)}, bf16[256,256]{1,0:T(8,128)(2,1)}, u32[]{:S(2)}) copy-start(bf16[256,256]{1,0:T(8,128)(2,1)} %constant.127.clone.refs_5_) | copy-start | bytes 393220
  283.6 30.9 %copy-start.10 = (bf16[256,256]{1,0:T(8,128)(2,1)S(1)}, bf16[256,256]{1,0:T(8,128)(2,1)}, u32[]{:S(2)}) copy-start(bf16[256,256]{1,0:T(8,128)(2,1)} %constant.128.clone.refs_6_) | copy-start | bytes 393220
  283.6 30.9 %copy-start.11 = (bf16[256,256]{1,0:T(8,128)(2,1)S(1)}, bf16[256,256]{1,0:T(8,128)(2,1)}, u32[]{:S(2)}) copy-start(bf16[256,256]{1,0:T(8,128)(2,1)} %constant.129.clone.refs_7_) | copy-start | bytes 393220
  283.6 30.9 %copy-start.12 = (bf16[256,256]{1,0:T(8,128)(2,1)S(1)}, bf16[256,256]{1,0:T(8,128)(2,1)}, u32[]{:S(2)}) copy-start(bf16[256,256]{1,0:T(8,128)(2,1)} %constant.132.clone.refs_10_) | copy-start | bytes 393220
  283.6 30.9 %copy-start.13 = (bf16[256,256]{1,0:T(8,128)(2,1)S(1)}, bf16[256,256]{1,0:T(8,128)(2,1)}, u32[]{:S(2)}) copy-start(bf16[256,256]{1,0:T(8,128)(2,1)} %constant.133.clone.refs_11_) | copy-start | bytes 393220
  283.6 30.9 %copy-start.14 = (bf16[256,256]{1,0:T(8,128)(2,1)S(1)}, bf16[256,256]{1,0:T(8,128)(2,1)}, u32[]{:S(2)}) copy-start(bf16[256,256]{1,0:T(8,128)(2,1)} %constant.134.clone.refs_12_) | copy-start | bytes 393220
  283.6 30.9 %copy-start.15 = (bf16[256,256]{1,0:T(8,128)(2,1)S(1)}, bf16[256,256]{1,0:T(8,128)(2,1)}, u32[]{:S(2)}) copy-start(bf16[256,256]{1,0:T(8,128)(2,1)} %constant.135.clone.refs_13_) | copy-start | bytes 393220
  312.3 2.0 copy-start.23
  327.3 47.0 %collective-permute-start.6 = (f32[128,1024]{1,0:T(8,128)S(1)}, f32[128,1024]{1,0:T(8,128)S(1)}, u32[]{:S(2)}, u32[]{:S(2)}) collective-permute-start(f32[128,1024]{1,0:T(8,128)S(1)} %shard_map.232), channel_id=1, source_target_pairs={{0,0},{4,1},{1,2},{5,3},{2,4},{6,5},{3,6},{7,7},{8,8},{12,9},{9,10... | collective-permute-start | bytes 1572872 | tf_op jit(solution)/shard_map/ppermute | solution.py:312
  369.9 18.4 %collective-permute-start.8 = (f32[128,1024]{1,0:T(8,128)S(1)}, f32[128,1024]{1,0:T(8,128)S(1)}, u32[]{:S(2)}, u32[]{:S(2)}) collective-permute-start(f32[128,1024]{1,0:T(8,128)S(1)} %shard_map.235), channel_id=1, source_target_pairs={{0,0},{4,1},{1,2},{5,3},{2,4},{6,5},{3,6},{7,7},{8,8},{12,9},{9,10... | collective-permute-start | bytes 1572872 | tf_op jit(solution)/shard_map/ppermute | solution.py:312
  (3 other events, 5.8 us)

commit v4 on v3

--- a/solution.py
+++ b/solution.py
@@ -112,10 +112,6 @@
     return re * gain, im * gain
 
 
-def times(a, b):
-    return a[0] * b[0] - a[1] * b[1], a[1] * b[0] + a[0] * b[1]
-
-
 def lane_is(shape, lane):
     return lax.broadcasted_iota(jnp.int32, shape, 1) == lane
 
@@ -144,7 +140,7 @@
     column[...] = middles
 
 
-def pair_kernel(turn, own, other, own_col, other_col, turn_row, *refs):
+def pair_kernel(own, other, own_col, other_col, *refs):
     (ah, al, zh, zl), back = refs[:4], refs[4:14]
     surface, spec, column = refs[14:]
     b0h, b0l, b2h, b2l, b1h, b1l, rh, rl, bzh, bzl = back
@@ -159,11 +155,7 @@
         for lane in range(0, along // 2, LANES):
             lanes = slice(lane, lane + LANES)
             load = lambda held: [(held[z, re_rows, lanes], held[z, im_rows, lanes]) for z in range(depth)]
-            theirs = [
-                times(point, (turn[0, u], turn[1, u]))
-                for u, point in enumerate(fft(load(other), -1))
-            ]
-            white = [whiten(a, b) for a, b in zip(fft(load(own), -1), theirs)]
+            white = [whiten(a, b) for a, b in zip(fft(load(own), -1), fft(load(other), -1))]
             for z, (re, im) in enumerate(fft(white, 1)):
                 spec[z, re_rows, lanes] = re
                 spec[z, im_rows, lanes] = im
@@ -176,8 +168,7 @@
         turned = by_right(jnp.concatenate((turned[:across], turned[across:]), axis=1), zh, zl)
         return turned[:, :LANES], turned[:, LANES:]
 
-    theirs = times(edge(other_col), (turn_row[0:1, :], turn_row[1:2, :]))
-    white = whiten(edge(own_col), theirs)
+    white = whiten(edge(own_col), edge(other_col))
     back_z = by_right(jnp.concatenate(white, axis=1), bzh, bzl)
     back_z = jnp.concatenate((back_z[:, :LANES], back_z[:, LANES:]), axis=0)
     column[...] = by_left(rh.at[:across], rl.at[:across], back_z)
@@ -240,15 +231,14 @@
     )(strip, *forth[:8])
 
 
-def pair_of(turn, own, other, forth, back):
+def pair_of(own, other, forth, back):
     depth, rows, half = own[0].shape
     across, along = rows // 2, 2 * half
-    row = jnp.pad(turn, ((0, 0), (0, LANES - depth)))
-    operands = [own[0], other[0], own[1], other[1], row] + forth[6:10] + back
+    operands = [own[0], other[0], own[1], other[1]] + forth[6:10] + back
     return pl.pallas_call(
         pair_kernel,
         out_shape=jax.ShapeDtypeStruct((across, along), F32),
-        in_specs=[pl.BlockSpec(memory_space=pltpu.SMEM)] + [VMEM] * len(operands),
+        in_specs=[VMEM] * len(operands),
         out_specs=VMEM,
         scratch_shapes=[
             pltpu.VMEM((depth, rows, half), F32),
@@ -258,62 +248,123 @@
         cost_estimate=pl.CostEstimate(
             flops=12 * 10**9, bytes_accessed=36 * 10**6, transcendentals=0
         ),
-    )(turn, *operands)
+    )(*operands)
+
+
+def work_place(t, slabs):
+    inside = t % (PER_CHIP * slabs)
+    return t // (PER_CHIP * slabs) * PER_CHIP + inside % PER_CHIP, inside // PER_CHIP
+
+
+def exchange_kernel(slabs, stored, band, send_sems, recv_sems, local_sem):
+    tile, slab = lax.axis_index("tile"), lax.axis_index("slab")
+    here = tile // PER_CHIP * PER_CHIP * slabs + slab * PER_CHIP + tile % PER_CHIP
+    home = here // slabs
+    stays = home == tile
+    barrier = pltpu.get_barrier_semaphore()
+
+    def signal(j):
+        pl.semaphore_signal(
+            barrier, inc=1, device_id=(home, j), device_id_type=pl.DeviceIdType.MESH
+        )
+
+    for j in range(slabs):
+        pl.when(jnp.logical_not(jnp.logical_and(stays, slab == j)))(lambda j=j: signal(j))
+    pl.semaphore_wait(barrier, slabs - stays.astype(jnp.int32))
+
+    local = pltpu.make_async_copy(stored.at[here % slabs], band.at[slab], local_sem)
+    pl.when(stays)(local.start)
+    copies = []
+    for step in range(slabs):
+        inside = (slab + step) % slabs
+        to = work_place(tile * slabs + inside, slabs)
+        copy = pltpu.make_async_remote_copy(
+            src_ref=stored.at[inside],
+            dst_ref=band.at[slab],
+            send_sem=send_sems.at[step],
+            recv_sem=recv_sems.at[slab],
+            device_id=to,
+            device_id_type=pl.DeviceIdType.MESH,
+        )
+        away = jnp.logical_not(jnp.logical_and(to[0] == tile, to[1] == slab))
+        pl.when(away)(copy.start)
+        copies.append((away, copy))
+    for away, copy in copies:
+        pl.when(away)(copy.wait_send)
+    for j in range(slabs):
+        arriving = pltpu.make_async_remote_copy(
+            src_ref=stored.at[0],
+            dst_ref=band.at[j],
+            send_sem=send_sems.at[0],
+            recv_sem=recv_sems.at[j],
+            device_id=(home, j),
+            device_id_type=pl.DeviceIdType.MESH,
+        )
+        pl.when(jnp.logical_not(jnp.logical_and(stays, slab == j)))(arriving.wait_recv)
+    pl.when(stays)(local.wait)
+
+
+def exchange(stored):
+    slabs = lax.axis_size("slab")
+    _, per, rows, along = stored.shape
+    band = pl.pallas_call(
+        lambda *refs: exchange_kernel(slabs, *refs),
+        out_shape=jax.ShapeDtypeStruct((slabs, per, rows, along), F32),
+        in_specs=[pl.BlockSpec(memory_space=pl.ANY)],
+        out_specs=pl.BlockSpec(memory_space=pl.ANY),
+        scratch_shapes=[
+            pltpu.SemaphoreType.DMA((slabs,)),
+            pltpu.SemaphoreType.DMA((slabs,)),
+            pltpu.SemaphoreType.DMA,
+        ],
+        compiler_params=pltpu.CompilerParams(
+            collective_id=0, has_side_effects=True, vmem_limit_bytes=48 * 1024 * 1024
+        ),
+        cost_estimate=pl.CostEstimate(
+            flops=0, bytes_accessed=2 * stored.size * 4, transcendentals=0
+        ),
+    )(stored)
+    return band.reshape(slabs * per, rows, along)
 
 
 def on_device(stored, offsets):
     axes = ("tile", "slab")
     slabs = lax.axis_size("slab")
     count = lax.axis_size(axes)
-    group = PER_CHIP * slabs
     per, along = stored.shape[1], stored.shape[3]
-    depth = per * slabs
-    forth, back = make_tables(depth, A, along)
+    forth, back = make_tables(per * slabs, A, along)
     strides = (1, GC)
 
     def place_of(t):
-        inside = t % group
-        return (t // group * PER_CHIP + inside % PER_CHIP) * slabs + inside // PER_CHIP
+        to = work_place(t, slabs)
+        return to[0] * slabs + to[1]
 
     def gives(rnd, t):
         to = t - strides[rnd]
         return to >= 0 and (rnd == 1 or to % GC != GC - 1)
 
-    def holder(t, step):
-        return t // slabs * slabs + (t - step) % slabs
-
     near = [(t, t - strides[1 - t % 2]) for t in range(count) if gives(1 - t % 2, t)]
     far = [(t, t - strides[t % 2]) for t in range(count) if gives(t % 2, t)]
 
     tile, slab = lax.axis_index("tile"), lax.axis_index("slab")
     odd = tile % PER_CHIP
     mine = lax.ppermute(offsets[:, :, 0], axes, [(t, place_of(t)) for t in range(count)])
-    bands = []
-    for step in range(slabs):
-        planes = lax.dynamic_index_in_dim(stored, (slab + step) % slabs, 0, False)
-        pairs = [(holder(t, step), place_of(t)) for t in range(count)]
-        bands.append(lax.ppermute(planes, axes, pairs))
+    band = exchange(stored)
 
     def cut(rnd, which):
-        return jnp.concatenate(
-            [lax.dynamic_slice_in_dim(band, mine[rnd, which], A, 1) for band in bands[::-1]]
-        )
+        return lax.dynamic_slice_in_dim(band, mine[rnd, which], A, 1)
 
     def arrive(strip, pairs):
         return lax.ppermute(strip, axes, [(place_of(t), place_of(to)) for t, to in pairs])
 
-    angles = [phases(np.arange(depth), [per * stride], depth) for stride in strides]
-    turns = jnp.asarray(np.stack([[c[:, 0], -s[:, 0]] for c, s in angles]), F32)
-
     def surface_of(rnd, strip):
         own = spectrum_of(cut(rnd, 0), per, forth)
-        turn = lax.dynamic_index_in_dim(turns, rnd, 0, False)
-        surface = pair_of(turn, own, spectrum_of(strip, per, forth), forth, back)
+        surface = pair_of(own, spectrum_of(strip, per, forth), forth, back)
         return lax.ppermute(surface, axes, [(place_of(t), t) for t in range(count)])
 
     given_far, given_near = cut(odd, 1), cut(1 - odd, 1)
+    strip_far = arrive(given_far, far)
     strip_near = arrive(given_near, near)
-    strip_far = arrive(given_far, far)
     from_near = surface_of(odd, strip_near)
     from_far = surface_of(1 - odd, strip_far)
     home_odd = (tile * slabs + slab) % 2 == 1

time: 392 us -> 356 us (0.908)
  the two profiles are of different devices: /device:TPU:28 before, /device:TPU:1 now
where the time goes in v4:
time: 356 us
  Pallas kernels  235 us (66%)
  waiting for transfers between devices  77.5 us (22%)
  local copies, waits for them, and re-layouts  20.4 us (6%)
  starting transfers between devices  12.6 us (4%)
  between operations  8.78 us (2%)
    pallas_call x1, Pallas kernels, exchange(): pl.pallas_call(lambda *refs: exchange_kernel(slabs, *refs), out_shape=jax...  184 us
    ppermute x2, waiting for transfers between devices, arrive(): lax.ppermute(strip, axes, [(place_of(t), place_of(to)) for t, to in pairs])  64.5 us
    pallas_call x4, Pallas kernels, spectrum_of(): pl.pallas_call(spectrum_kernel, grid=(depth // per,), out_shape=(jax.Shap...  25.8 us
    pallas_call x2, Pallas kernels, pair_of(): pl.pallas_call(pair_kernel, out_shape=jax.ShapeDtypeStruct((across, along...  24.7 us
    ppermute x2, waiting for transfers between devices, surface_of(): return lax.ppermute(surface, axes, [(place_of(t), t) for t in range(count)])  12.9 us
    dynamic_slice x2, local copies, waits for them, and re-layouts, cut(): return lax.dynamic_slice_in_dim(band, mine[rnd, which], A, 1)  12.4 us
    unnamed x48, local copies, waits for them, and re-layouts  8 us
  transfers between devices with their start and end apart: 5, of which 2 were waited for; matrix products, arithmetic and copies ran while one was open for 0% of the time, Pallas kernels for 66%

profile of v4, /device:TPU:1, one launch (start us, length us, event | category | flops | bytes accessed | tf_op | source)
XLA Modules:
  0.0 355.7 jit_solution(9140680889977664938)
XLA Ops:
  0.6 5.6 %collective-permute-start = (s32[2,2]{1,0:T(2,128)}, s32[2,2]{1,0:T(2,128)S(1)}, u32[]{:S(2)}, u32[]{:S(2)}) collective-permute-start(s32[2,2]{1,0:T(2,128)} %bitcast.17), channel_id=1, source_target_pairs={{0,0},{1,4},{2,1},{3,5},{4,2},{5,6},{6,3},{7,7},{8,8},{9,12},{10,9... | collective-permute-start | bytes 56 | tf_op jit(solution)/shard_map/ppermute | solution.py:351
  6.3 184.1 %shard_map.221 = f32[4,2,256,1024]{3,2,1,0:T(8,128)} custom-call(f32[4,2,256,1024]{3,2,1,0:T(8,128)} %refs_0_.3), custom_call_target="tpu_custom_call" | custom-call | bytes 16777216 | tf_op jit(solution)/shard_map/pallas_call | solution.py:310
  190.4 0.6 constant_dynamic-slice_fusion.7
  198.7 0.0 copy-start.2
  198.7 0.0 copy-start.4
  198.8 0.0 copy-start.5
  198.8 0.0 copy-start.16
  198.8 0.0 copy-start.17
  198.8 0.0 copy-start.18
  198.8 0.0 copy-start.19
  198.8 11.8 %constant_dynamic-slice_fusion.3 = (f32[8,128,1024]{2,1,0:T(8,128)}, f32[8,128,1024]{2,1,0:T(8,128)S(1)}, f32[8,128,1024]{2,1,0:T(8,128)}, f32[8,128,1024]{2,1,0:T(8,128)}) fusion(f32[8,256,1024]{2,1,0:T(8,128)} %bitcast.15, s32[]{:T(128)S(6)} %select_n.49, s32[]{:T(128)S(6)} %select_n.51, s32[]{:T(128)S(6)} %select_n.50, s32[]{:T(128)S(6)} %select_n.47), kind=kLoop, calls=%fused_computation.8 | loop fusion | bytes 33554448 | tf_op jit(solution)/shard_map/dynamic_slice | solution.py:355
  210.6 1.3 collective-permute-start.1
  211.9 1.9 collective-permute-start.3
  213.9 6.5 %shard_map.225 = (f32[8,256,512]{2,1,0:T(8,128)S(1)}, f32[128,128]{1,0:T(8,128)S(1)}) custom-call(f32[8,128,1024]{2,1,0:T(8,128)} %get-tuple-element.22.strip, bf16[256,256]{1,0:T(8,128)(2,1)S(1)} %copy-done.19, bf16[256,256]{1,0:T(8,128)(2,1)S(1)} %copy-done.18, bf16[256,256]{1,0:T(8,128)(2,1)S(1)} %copy-done.17, bf16[256,256]{1,0:T(8,128)(2,1)S(1)} %copy-done.16, ...), custom_call_target="tpu_custom_call" | custom-call | flops 6000000000 | bytes 10000000 | tf_op jit(solution)/shard_map/pallas_call | solution.py:214
  220.4 1.9 copy-done.20
  222.4 6.5 %shard_map.222 = (f32[8,256,512]{2,1,0:T(8,128)S(1)}, f32[128,128]{1,0:T(8,128)S(1)}) custom-call(f32[8,128,1024]{2,1,0:T(8,128)} %get-tuple-element.23.strip, bf16[256,256]{1,0:T(8,128)(2,1)S(1)} %copy-done.19, bf16[256,256]{1,0:T(8,128)(2,1)S(1)} %copy-done.18, bf16[256,256]{1,0:T(8,128)(2,1)S(1)} %copy-done.17, bf16[256,256]{1,0:T(8,128)(2,1)S(1)} %copy-done.16, ...), custom_call_target="tpu_custom_call" | custom-call | flops 6000000000 | bytes 10000000 | tf_op jit(solution)/shard_map/pallas_call | solution.py:214
  228.8 1.9 copy-done.22
  230.8 0.0 copy-start.9
  230.8 0.0 copy-start.10
  230.8 0.0 copy-start.11
  230.9 64.5 %collective-permute-done.1.strip = f32[8,128,1024]{2,1,0:T(8,128)} collective-permute-done((f32[8,128,1024]{2,1,0:T(8,128)}, f32[8,128,1024]{2,1,0:T(8,128)}, u32[]{:S(2)}, u32[]{:S(2)}) %collective-permute-start.1) | collective-permute-done | bytes 4194336 | tf_op jit(solution)/shard_map/ppermute | solution.py:358
  295.4 6.5 %shard_map.223 = (f32[8,256,512]{2,1,0:T(8,128)S(1)}, f32[128,128]{1,0:T(8,128)S(1)}) custom-call(f32[8,128,1024]{2,1,0:T(8,128)} %collective-permute-done.1.strip, bf16[256,256]{1,0:T(8,128)(2,1)S(1)} %copy-done.19, bf16[256,256]{1,0:T(8,128)(2,1)S(1)} %copy-done.18, bf16[256,256]{1,0:T(8,128)(2,1)S(1)} %copy-done.17, bf16[256,256]{1,0:T(8,128)(2,1)S(1)} %copy-done.16, ...), custom_call_target="tpu_custom_call" | custom-call | flops 6000000000 | bytes 10000000 | tf_op jit(solution)/shard_map/pallas_call | solution.py:214
  301.9 2.0 copy-done.23
  304.0 12.4 %shard_map.224 = f32[128,1024]{1,0:T(8,128)S(1)} custom-call(f32[8,256,512]{2,1,0:T(8,128)} %copy-done.22, f32[8,256,512]{2,1,0:T(8,128)} %copy-done.23, f32[128,128]{1,0:T(8,128)S(1)} %get-tuple-element.12.own_col, f32[128,128]{1,0:T(8,128)S(1)} %get-tuple-element.13.other_col, bf16[256,256]{1,0:T(8,128)(2,1)S(1)} %copy-done.5, ...), custom_call_target="tpu_custom_call" | custom-call | flops 12000000000 | bytes 36000000 | tf_op jit(solution)/shard_map/pallas_call | solution.py:238
  316.3 1.9 collective-permute-start.2
  318.3 6.5 %shard_map.226 = (f32[8,256,512]{2,1,0:T(8,128)S(1)}, f32[128,128]{1,0:T(8,128)S(1)}) custom-call(f32[8,128,1024]{2,1,0:T(8,128)} %collective-permute-done.3.strip, bf16[256,256]{1,0:T(8,128)(2,1)S(1)} %copy-done.19, bf16[256,256]{1,0:T(8,128)(2,1)S(1)} %copy-done.18, bf16[256,256]{1,0:T(8,128)(2,1)S(1)} %copy-done.17, bf16[256,256]{1,0:T(8,128)(2,1)S(1)} %copy-done.16, ...), custom_call_target="tpu_custom_call" | custom-call | flops 6000000000 | bytes 10000000 | tf_op jit(solution)/shard_map/pallas_call | solution.py:214
  324.8 2.0 copy-done.21
  326.8 12.4 %shard_map.227 = f32[128,1024]{1,0:T(8,128)S(1)} custom-call(f32[8,256,512]{2,1,0:T(8,128)} %copy-done.20, f32[8,256,512]{2,1,0:T(8,128)} %copy-done.21, f32[128,128]{1,0:T(8,128)S(1)} %get-tuple-element.16.own_col, f32[128,128]{1,0:T(8,128)S(1)} %get-tuple-element.17.other_col, bf16[256,256]{1,0:T(8,128)(2,1)S(1)} %copy-done.5, ...), custom_call_target="tpu_custom_call" | custom-call | flops 12000000000 | bytes 36000000 | tf_op jit(solution)/shard_map/pallas_call | solution.py:238
  339.1 1.9 collective-permute-start.4
  341.1 12.9 %collective-permute-done.4 = f32[128,1024]{1,0:T(8,128)S(1)} collective-permute-done((f32[128,1024]{1,0:T(8,128)S(1)}, f32[128,1024]{1,0:T(8,128)S(1)}, u32[]{:S(2)}, u32[]{:S(2)}) %collective-permute-start.4) | collective-permute-done | bytes 524320 | tf_op jit(solution)/shard_map/ppermute | solution.py:363
  354.0 0.1 select_bitcast_fusion.1
  354.1 1.6 fusion
  (37 shorter events, 0.1 us)
Async XLA Ops:
  0.6 189.8 %collective-permute-start = (s32[2,2]{1,0:T(2,128)}, s32[2,2]{1,0:T(2,128)S(1)}, u32[]{:S(2)}, u32[]{:S(2)}) collective-permute-start(s32[2,2]{1,0:T(2,128)} %bitcast.17), channel_id=1, source_target_pairs={{0,0},{1,4},{2,1},{3,5},{4,2},{5,6},{6,3},{7,7},{8,8},{9,12},{10,9... | collective-permute-start | bytes 56 | tf_op jit(solution)/shard_map/ppermute | solution.py:351
  198.7 15.1 %copy-start.2 = (bf16[512,512]{1,0:T(8,128)(2,1)S(1)}, bf16[512,512]{1,0:T(8,128)(2,1)}, u32[]{:S(2)}) copy-start(bf16[512,512]{1,0:T(8,128)(2,1)} %constant.81.clone.f1l) | copy-start | bytes 1572868
  198.7 15.1 %copy-start.3 = (bf16[512,512]{1,0:T(8,128)(2,1)S(1)}, bf16[512,512]{1,0:T(8,128)(2,1)}, u32[]{:S(2)}) copy-start(bf16[512,512]{1,0:T(8,128)(2,1)} %constant.80.clone.f1h) | copy-start | bytes 1572868
  198.7 15.1 %copy-start.4 = (bf16[256,256]{1,0:T(8,128)(2,1)S(1)}, bf16[256,256]{1,0:T(8,128)(2,1)}, u32[]{:S(2)}) copy-start(bf16[256,256]{1,0:T(8,128)(2,1)} %constant.83.clone.rl.refs_1_) | copy-start | bytes 393220
  198.8 15.1 %copy-start.5 = (bf16[256,256]{1,0:T(8,128)(2,1)S(1)}, bf16[256,256]{1,0:T(8,128)(2,1)}, u32[]{:S(2)}) copy-start(bf16[256,256]{1,0:T(8,128)(2,1)} %constant.82.clone.rh.refs_0_) | copy-start | bytes 393220
  198.8 15.1 %copy-start.16 = (bf16[256,256]{1,0:T(8,128)(2,1)S(1)}, bf16[256,256]{1,0:T(8,128)(2,1)}, u32[]{:S(2)}) copy-start(bf16[256,256]{1,0:T(8,128)(2,1)} %constant.79.clone.f2l) | copy-start | bytes 393220
  198.8 15.1 %copy-start.17 = (bf16[256,256]{1,0:T(8,128)(2,1)S(1)}, bf16[256,256]{1,0:T(8,128)(2,1)}, u32[]{:S(2)}) copy-start(bf16[256,256]{1,0:T(8,128)(2,1)} %constant.78.clone.f2h) | copy-start | bytes 393220
  198.8 15.1 %copy-start.18 = (bf16[256,256]{1,0:T(8,128)(2,1)S(1)}, bf16[256,256]{1,0:T(8,128)(2,1)}, u32[]{:S(2)}) copy-start(bf16[256,256]{1,0:T(8,128)(2,1)} %constant.77.clone.f0l) | copy-start | bytes 393220
  198.8 15.1 %copy-start.19 = (bf16[256,256]{1,0:T(8,128)(2,1)S(1)}, bf16[256,256]{1,0:T(8,128)(2,1)}, u32[]{:S(2)}) copy-start(bf16[256,256]{1,0:T(8,128)(2,1)} %constant.76.clone.f0h) | copy-start | bytes 393220
  210.6 84.8 %collective-permute-start.1 = (f32[8,128,1024]{2,1,0:T(8,128)}, f32[8,128,1024]{2,1,0:T(8,128)}, u32[]{:S(2)}, u32[]{:S(2)}) collective-permute-start(f32[8,128,1024]{2,1,0:T(8,128)} %get-tuple-element.20), channel_id=1, source_target_pairs={{1,4},{2,5},{3,6},{7,0},{8,7},{12,1},{9,12},{13,2},{10,13},{14,3},... | collective-permute-start | bytes 12582920 | tf_op jit(solution)/shard_map/ppermute | solution.py:358
  211.9 106.3 %collective-permute-start.3 = (f32[8,128,1024]{2,1,0:T(8,128)S(1)}, f32[8,128,1024]{2,1,0:T(8,128)}, u32[]{:S(2)}, u32[]{:S(2)}) collective-permute-start(f32[8,128,1024]{2,1,0:T(8,128)S(1)} %get-tuple-element.21), channel_id=1, source_target_pairs={{4,0},{5,1},{6,2},{8,4},{12,8},{9,5},{13,9},{10,6},{14,10},{11,7},... | collective-permute-start | bytes 12582920 | tf_op jit(solution)/shard_map/ppermute | solution.py:358
  220.4 2.0 copy-start.20
  228.8 1.9 copy-start.22
  230.8 73.1 %copy-start = (bf16[512,512]{1,0:T(8,128)(2,1)S(1)}, bf16[512,512]{1,0:T(8,128)(2,1)}, u32[]{:S(2)}) copy-start(bf16[512,512]{1,0:T(8,128)(2,1)} %constant.91.clone.refs_9_) | copy-start | bytes 1572868
  230.8 73.1 %copy-start.1 = (bf16[512,512]{1,0:T(8,128)(2,1)S(1)}, bf16[512,512]{1,0:T(8,128)(2,1)}, u32[]{:S(2)}) copy-start(bf16[512,512]{1,0:T(8,128)(2,1)} %constant.90.clone.refs_8_) | copy-start | bytes 1572868
  230.8 73.1 %copy-start.6 = (bf16[256,256]{1,0:T(8,128)(2,1)S(1)}, bf16[256,256]{1,0:T(8,128)(2,1)}, u32[]{:S(2)}) copy-start(bf16[256,256]{1,0:T(8,128)(2,1)} %constant.95.clone.refs_13_) | copy-start | bytes 393220
  230.8 73.1 %copy-start.7 = (bf16[256,256]{1,0:T(8,128)(2,1)S(1)}, bf16[256,256]{1,0:T(8,128)(2,1)}, u32[]{:S(2)}) copy-start(bf16[256,256]{1,0:T(8,128)(2,1)} %constant.94.clone.refs_12_) | copy-start | bytes 393220
  230.8 73.1 %copy-start.8 = (bf16[256,256]{1,0:T(8,128)(2,1)S(1)}, bf16[256,256]{1,0:T(8,128)(2,1)}, u32[]{:S(2)}) copy-start(bf16[256,256]{1,0:T(8,128)(2,1)} %constant.93.clone.refs_11_) | copy-start | bytes 393220
  230.8 73.1 %copy-start.9 = (bf16[256,256]{1,0:T(8,128)(2,1)S(1)}, bf16[256,256]{1,0:T(8,128)(2,1)}, u32[]{:S(2)}) copy-start(bf16[256,256]{1,0:T(8,128)(2,1)} %constant.92.clone.refs_10_) | copy-start | bytes 393220
  230.8 73.1 %copy-start.10 = (bf16[256,256]{1,0:T(8,128)(2,1)S(1)}, bf16[256,256]{1,0:T(8,128)(2,1)}, u32[]{:S(2)}) copy-start(bf16[256,256]{1,0:T(8,128)(2,1)} %constant.89.clone.refs_7_) | copy-start | bytes 393220
  230.8 73.1 %copy-start.11 = (bf16[256,256]{1,0:T(8,128)(2,1)S(1)}, bf16[256,256]{1,0:T(8,128)(2,1)}, u32[]{:S(2)}) copy-start(bf16[256,256]{1,0:T(8,128)(2,1)} %constant.88.clone.refs_6_) | copy-start | bytes 393220
  230.8 73.1 %copy-start.12 = (bf16[256,256]{1,0:T(8,128)(2,1)S(1)}, bf16[256,256]{1,0:T(8,128)(2,1)}, u32[]{:S(2)}) copy-start(bf16[256,256]{1,0:T(8,128)(2,1)} %constant.87.clone.refs_5_) | copy-start | bytes 393220
  230.8 73.1 %copy-start.13 = (bf16[256,256]{1,0:T(8,128)(2,1)S(1)}, bf16[256,256]{1,0:T(8,128)(2,1)}, u32[]{:S(2)}) copy-start(bf16[256,256]{1,0:T(8,128)(2,1)} %constant.86.clone.refs_4_) | copy-start | bytes 393220
  230.8 73.1 %copy-start.14 = (bf16[256,256]{1,0:T(8,128)(2,1)S(1)}, bf16[256,256]{1,0:T(8,128)(2,1)}, u32[]{:S(2)}) copy-start(bf16[256,256]{1,0:T(8,128)(2,1)} %constant.85.clone.refs_3_) | copy-start | bytes 393220
  230.9 73.1 %copy-start.15 = (bf16[256,256]{1,0:T(8,128)(2,1)S(1)}, bf16[256,256]{1,0:T(8,128)(2,1)}, u32[]{:S(2)}) copy-start(bf16[256,256]{1,0:T(8,128)(2,1)} %constant.84.clone.refs_2_) | copy-start | bytes 393220
  301.9 2.0 copy-start.23
  316.3 24.7 %collective-permute-start.2 = (f32[128,1024]{1,0:T(8,128)S(1)}, f32[128,1024]{1,0:T(8,128)S(1)}, u32[]{:S(2)}, u32[]{:S(2)}) collective-permute-start(f32[128,1024]{1,0:T(8,128)S(1)} %shard_map.224), channel_id=1, source_target_pairs={{0,0},{4,1},{1,2},{5,3},{2,4},{6,5},{3,6},{7,7},{8,8},{12,9},{9,10... | collective-permute-start | bytes 1572872 | tf_op jit(solution)/shard_map/ppermute | solution.py:363
  324.7 2.0 copy-start.21
  339.1 14.9 %collective-permute-start.4 = (f32[128,1024]{1,0:T(8,128)S(1)}, f32[128,1024]{1,0:T(8,128)S(1)}, u32[]{:S(2)}, u32[]{:S(2)}) collective-permute-start(f32[128,1024]{1,0:T(8,128)S(1)} %shard_map.227), channel_id=1, source_target_pairs={{0,0},{4,1},{1,2},{5,3},{2,4},{6,5},{3,6},{7,7},{8,8},{12,9},{9,10... | collective-permute-start | bytes 1572872 | tf_op jit(solution)/shard_map/ppermute | solution.py:363

commit v5 on v4

--- a/solution.py
+++ b/solution.py
@@ -351,22 +351,26 @@
     mine = lax.ppermute(offsets[:, :, 0], axes, [(t, place_of(t)) for t in range(count)])
     band = exchange(stored)
 
-    def cut(rnd, which):
-        return lax.dynamic_slice_in_dim(band, mine[rnd, which], A, 1)
+    def cut(planes, rnd, which):
+        return lax.dynamic_slice_in_dim(planes, mine[rnd, which], A, 1)
 
     def arrive(strip, pairs):
         return lax.ppermute(strip, axes, [(place_of(t), place_of(to)) for t, to in pairs])
 
-    def surface_of(rnd, strip):
-        own = spectrum_of(cut(rnd, 0), per, forth)
-        surface = pair_of(own, spectrum_of(strip, per, forth), forth, back)
+    def send_home(surface):
         return lax.ppermute(surface, axes, [(place_of(t), t) for t in range(count)])
 
-    given_far, given_near = cut(odd, 1), cut(1 - odd, 1)
+    given_far, given_near = cut(band, odd, 1), cut(band, 1 - odd, 1)
+    band, given_far, given_near = lax.optimization_barrier((band, given_far, given_near))
     strip_far = arrive(given_far, far)
     strip_near = arrive(given_near, near)
-    from_near = surface_of(odd, strip_near)
-    from_far = surface_of(1 - odd, strip_far)
+    own_near = spectrum_of(cut(band, odd, 0), per, forth)
+    own_far = spectrum_of(cut(band, 1 - odd, 0), per, forth)
+    surface_near = pair_of(own_near, spectrum_of(strip_near, per, forth), forth, back)
+    from_near = send_home(surface_near)
+    strip_far, _ = lax.optimization_barrier((strip_far, surface_near))
+    surface_far = pair_of(own_far, spectrum_of(strip_far, per, forth), forth, back)
+    from_far = send_home(surface_far)
     home_odd = (tile * slabs + slab) % 2 == 1
     surface = jnp.stack(
         (jnp.where(home_odd, from_far, from_near), jnp.where(home_odd, from_near, from_far))

time: 356 us -> 385 us (1.081)
  waiting for transfers between devices: 77.5 us -> 26.7 us
  Pallas kernels: 235 us -> 280 us
  starting transfers between devices: 12.6 us -> 41.6 us
  local copies, waits for them, and re-layouts: 20.4 us -> 26.7 us
    ppermute x2, waiting for transfers between devices: 64.5 us -> 16.8 us  [arrive(): lax.ppermute(strip, axes, [(place_of(t), place_of(to)) for t, to in pairs])]
    pallas_call x1, Pallas kernels: 184 us -> 229 us  [exchange(): pl.pallas_call(lambda *refs: exchange_kernel(slabs, *refs), out_shape=jax...]
    ppermute x2, starting transfers between devices: 3.84 us -> 32.8 us  [send_home(): return lax.ppermute(surface, axes, [(place_of(t), t) for t in range(count)])]
    dynamic_slice x2 -> x3, local copies, waits for them, and re-layouts: 12.4 us -> 18.6 us  [cut(): return lax.dynamic_slice_in_dim(planes, mine[rnd, which], A, 1)]
  transfers between devices with their start and end apart: 5 -> 5, of which waited for: 2 -> 3; matrix products, arithmetic and copies ran while one was open for 0% -> 2% of each run, Pallas kernels for 66% -> 68%
where the time goes in v5:
time: 385 us
  Pallas kernels  280 us (73%)
  starting transfers between devices  41.6 us (11%)
  waiting for transfers between devices  26.7 us (7%)
  local copies, waits for them, and re-layouts  26.7 us (7%)
  between operations  8.5 us (2%)
    pallas_call x1, Pallas kernels, exchange(): pl.pallas_call(lambda *refs: exchange_kernel(slabs, *refs), out_shape=jax...  229 us
    ppermute x2, starting transfers between devices, send_home(): return lax.ppermute(surface, axes, [(place_of(t), t) for t in range(count)])  32.8 us
    pallas_call x4, Pallas kernels, spectrum_of(): pl.pallas_call(spectrum_kernel, grid=(depth // per,), out_shape=(jax.Shap...  25.8 us
    pallas_call x2, Pallas kernels, pair_of(): pl.pallas_call(pair_kernel, out_shape=jax.ShapeDtypeStruct((across, along...  24.7 us
    dynamic_slice x3, local copies, waits for them, and re-layouts, cut(): return lax.dynamic_slice_in_dim(planes, mine[rnd, which], A, 1)  18.6 us
    ppermute x2, waiting for transfers between devices, arrive(): lax.ppermute(strip, axes, [(place_of(t), place_of(to)) for t, to in pairs])  16.8 us
    ppermute x2, waiting for transfers between devices, send_home(): return lax.ppermute(surface, axes, [(place_of(t), t) for t in range(count)])  9.97 us
    unnamed x48, local copies, waits for them, and re-layouts  8.06 us
  transfers between devices with their start and end apart: 5, of which 3 were waited for; matrix products, arithmetic and copies ran while one was open for 2% of the time, Pallas kernels for 68%

profile of v5, /device:TPU:1, one launch (start us, length us, event | category | flops | bytes accessed | tf_op | source)
XLA Modules:
  0.0 384.9 jit_solution(5475259508230155739)
XLA Ops:
  0.6 5.6 %collective-permute-start = (s32[2,2]{1,0:T(2,128)}, s32[2,2]{1,0:T(2,128)S(1)}, u32[]{:S(2)}, u32[]{:S(2)}) collective-permute-start(s32[2,2]{1,0:T(2,128)} %bitcast.18), channel_id=1, source_target_pairs={{0,0},{1,4},{2,1},{3,5},{4,2},{5,6},{6,3},{7,7},{8,8},{9,12},{10,9... | collective-permute-start | bytes 56 | tf_op jit(solution)/shard_map/ppermute | solution.py:351
  6.3 229.1 %shard_map.221 = f32[4,2,256,1024]{3,2,1,0:T(8,128)} custom-call(f32[4,2,256,1024]{3,2,1,0:T(8,128)} %refs_0_.3), custom_call_target="tpu_custom_call" | custom-call | bytes 16777216 | tf_op jit(solution)/shard_map/pallas_call | solution.py:310
  235.4 0.6 constant_dynamic-slice_fusion.3
  239.5 9.0 %constant_dynamic-slice_fusion.4 = (f32[8,128,1024]{2,1,0:T(8,128)}, f32[8,128,1024]{2,1,0:T(8,128)}) fusion(f32[8,256,1024]{2,1,0:T(8,128)} %bitcast.15, s32[]{:T(128)S(6)} %select_n.49, s32[]{:T(128)S(6)} %select_n.47), kind=kLoop, calls=%fused_computation.9 | loop fusion | bytes 16777224 | tf_op jit(solution)/shard_map/dynamic_slice | solution.py:355
  248.5 1.9 collective-permute-start.2
  250.4 1.3 collective-permute-start.1
  255.6 0.0 copy-start.2
  255.6 0.0 copy-start.3
  255.6 0.0 copy-start.4
  255.6 0.0 copy-start.5
  255.6 0.0 copy-start.17
  255.7 0.0 copy-start.18
  255.7 0.0 copy-start.19
  255.7 9.1 %constant_dynamic-slice_fusion.2 = (f32[8,128,1024]{2,1,0:T(8,128)}, f32[8,128,1024]{2,1,0:T(8,128)}) fusion(f32[8,256,1024]{2,1,0:T(8,128)} %bitcast.16, s32[]{:T(128)S(6)} %select_n.50, s32[]{:T(128)S(6)} %select_n.51), kind=kLoop, calls=%fused_computation.7 | loop fusion | bytes 16777224 | tf_op jit(solution)/shard_map/dynamic_slice | solution.py:355
  264.8 6.5 %shard_map.222 = (f32[8,256,512]{2,1,0:T(8,128)S(1)}, f32[128,128]{1,0:T(8,128)S(1)}) custom-call(f32[8,128,1024]{2,1,0:T(8,128)} %get-tuple-element.28.strip, bf16[256,256]{1,0:T(8,128)(2,1)S(1)} %copy-done.19, bf16[256,256]{1,0:T(8,128)(2,1)S(1)} %copy-done.18, bf16[256,256]{1,0:T(8,128)(2,1)S(1)} %copy-done.17, bf16[256,256]{1,0:T(8,128)(2,1)S(1)} %copy-done.16, ...), custom_call_target="tpu_custom_call" | custom-call | flops 6000000000 | bytes 10000000 | tf_op jit(solution)/shard_map/pallas_call | solution.py:214
  271.3 2.0 copy-done.20
  273.3 6.5 %shard_map.223 = (f32[8,256,512]{2,1,0:T(8,128)S(1)}, f32[128,128]{1,0:T(8,128)S(1)}) custom-call(f32[8,128,1024]{2,1,0:T(8,128)} %get-tuple-element.29.strip, bf16[256,256]{1,0:T(8,128)(2,1)S(1)} %copy-done.19, bf16[256,256]{1,0:T(8,128)(2,1)S(1)} %copy-done.18, bf16[256,256]{1,0:T(8,128)(2,1)S(1)} %copy-done.17, bf16[256,256]{1,0:T(8,128)(2,1)S(1)} %copy-done.16, ...), custom_call_target="tpu_custom_call" | custom-call | flops 6000000000 | bytes 10000000 | tf_op jit(solution)/shard_map/pallas_call | solution.py:214
  279.7 2.0 copy-done.22
  281.7 0.0 copy-start.8
  281.8 16.8 %collective-permute-done.2.strip = f32[8,128,1024]{2,1,0:T(8,128)} collective-permute-done((f32[8,128,1024]{2,1,0:T(8,128)}, f32[8,128,1024]{2,1,0:T(8,128)}, u32[]{:S(2)}, u32[]{:S(2)}) %collective-permute-start.2) | collective-permute-done | bytes 4194336 | tf_op jit(solution)/shard_map/ppermute | solution.py:358
  298.6 6.5 %shard_map.224 = (f32[8,256,512]{2,1,0:T(8,128)S(1)}, f32[128,128]{1,0:T(8,128)S(1)}) custom-call(f32[8,128,1024]{2,1,0:T(8,128)} %collective-permute-done.2.strip, bf16[256,256]{1,0:T(8,128)(2,1)S(1)} %copy-done.19, bf16[256,256]{1,0:T(8,128)(2,1)S(1)} %copy-done.18, bf16[256,256]{1,0:T(8,128)(2,1)S(1)} %copy-done.17, bf16[256,256]{1,0:T(8,128)(2,1)S(1)} %copy-done.16, ...), custom_call_target="tpu_custom_call" | custom-call | flops 6000000000 | bytes 10000000 | tf_op jit(solution)/shard_map/pallas_call | solution.py:214
  305.1 2.0 copy-done.23
  307.1 12.4 %shard_map.225 = f32[128,1024]{1,0:T(8,128)S(1)} custom-call(f32[8,256,512]{2,1,0:T(8,128)} %copy-done.22, f32[8,256,512]{2,1,0:T(8,128)} %copy-done.23, f32[128,128]{1,0:T(8,128)S(1)} %get-tuple-element.20.own_col, f32[128,128]{1,0:T(8,128)S(1)} %get-tuple-element.21.other_col, bf16[256,256]{1,0:T(8,128)(2,1)S(1)} %copy-done.5, ...), custom_call_target="tpu_custom_call" | custom-call | flops 12000000000 | bytes 36000000 | tf_op jit(solution)/shard_map/pallas_call | solution.py:238
  319.5 6.5 %shard_map.226 = (f32[8,256,512]{2,1,0:T(8,128)S(1)}, f32[128,128]{1,0:T(8,128)S(1)}) custom-call(f32[8,128,1024]{2,1,0:T(8,128)} %collective-permute-done.1.strip, bf16[256,256]{1,0:T(8,128)(2,1)S(1)} %copy-done.19, bf16[256,256]{1,0:T(8,128)(2,1)S(1)} %copy-done.18, bf16[256,256]{1,0:T(8,128)(2,1)S(1)} %copy-done.17, bf16[256,256]{1,0:T(8,128)(2,1)S(1)} %copy-done.16, ...), custom_call_target="tpu_custom_call" | custom-call | flops 6000000000 | bytes 10000000 | tf_op jit(solution)/shard_map/pallas_call | solution.py:214
  326.0 2.0 copy-done.21
  328.0 12.4 %shard_map.227 = f32[128,1024]{1,0:T(8,128)S(1)} custom-call(f32[8,256,512]{2,1,0:T(8,128)} %copy-done.20, f32[8,256,512]{2,1,0:T(8,128)} %copy-done.21, f32[128,128]{1,0:T(8,128)S(1)} %get-tuple-element.24.own_col, f32[128,128]{1,0:T(8,128)S(1)} %get-tuple-element.25.other_col, bf16[256,256]{1,0:T(8,128)(2,1)S(1)} %copy-done.5, ...), custom_call_target="tpu_custom_call" | custom-call | flops 12000000000 | bytes 36000000 | tf_op jit(solution)/shard_map/pallas_call | solution.py:238
  340.4 1.9 collective-permute-start.3
  342.3 30.9 %collective-permute-start.4 = (f32[128,1024]{1,0:T(8,128)S(1)}, f32[128,1024]{1,0:T(8,128)S(1)}, u32[]{:S(2)}, u32[]{:S(2)}) collective-permute-start(f32[128,1024]{1,0:T(8,128)S(1)} %shard_map.225), channel_id=1, source_target_pairs={{0,0},{4,1},{1,2},{5,3},{2,4},{6,5},{3,6},{7,7},{8,8},{12,9},{9,10... | collective-permute-start | bytes 1572872 | tf_op jit(solution)/shard_map/ppermute | solution.py:361
  373.2 4.4 %collective-permute-done.3 = f32[128,1024]{1,0:T(8,128)S(1)} collective-permute-done((f32[128,1024]{1,0:T(8,128)S(1)}, f32[128,1024]{1,0:T(8,128)S(1)}, u32[]{:S(2)}, u32[]{:S(2)}) %collective-permute-start.3) | collective-permute-done | bytes 524320 | tf_op jit(solution)/shard_map/ppermute | solution.py:361
  377.6 5.6 %collective-permute-done.4 = f32[128,1024]{1,0:T(8,128)S(1)} collective-permute-done((f32[128,1024]{1,0:T(8,128)S(1)}, f32[128,1024]{1,0:T(8,128)S(1)}, u32[]{:S(2)}, u32[]{:S(2)}) %collective-permute-start.4) | collective-permute-done | bytes 524320 | tf_op jit(solution)/shard_map/ppermute | solution.py:361
  383.2 0.1 select_bitcast_fusion.1
  383.3 1.6 fusion
  (38 shorter events, 0.1 us)
Async XLA Ops:
  0.6 234.7 %collective-permute-start = (s32[2,2]{1,0:T(2,128)}, s32[2,2]{1,0:T(2,128)S(1)}, u32[]{:S(2)}, u32[]{:S(2)}) collective-permute-start(s32[2,2]{1,0:T(2,128)} %bitcast.18), channel_id=1, source_target_pairs={{0,0},{1,4},{2,1},{3,5},{4,2},{5,6},{6,3},{7,7},{8,8},{9,12},{10,9... | collective-permute-start | bytes 56 | tf_op jit(solution)/shard_map/ppermute | solution.py:351
  248.5 50.1 %collective-permute-start.2 = (f32[8,128,1024]{2,1,0:T(8,128)}, f32[8,128,1024]{2,1,0:T(8,128)}, u32[]{:S(2)}, u32[]{:S(2)}) collective-permute-start(f32[8,128,1024]{2,1,0:T(8,128)} %get-tuple-element.18), channel_id=1, source_target_pairs={{4,0},{5,1},{6,2},{8,4},{12,8},{9,5},{13,9},{10,6},{14,10},{11,7},... | collective-permute-start | bytes 12582920 | tf_op jit(solution)/shard_map/ppermute | solution.py:358
  250.4 69.1 %collective-permute-start.1 = (f32[8,128,1024]{2,1,0:T(8,128)}, f32[8,128,1024]{2,1,0:T(8,128)}, u32[]{:S(2)}, u32[]{:S(2)}) collective-permute-start(f32[8,128,1024]{2,1,0:T(8,128)} %get-tuple-element.16), channel_id=1, source_target_pairs={{1,4},{2,5},{3,6},{7,0},{8,7},{12,1},{9,12},{13,2},{10,13},{14,3},... | collective-permute-start | bytes 12582920 | tf_op jit(solution)/shard_map/ppermute | solution.py:358
  255.6 9.2 %copy-start.2 = (bf16[512,512]{1,0:T(8,128)(2,1)S(1)}, bf16[512,512]{1,0:T(8,128)(2,1)}, u32[]{:S(2)}) copy-start(bf16[512,512]{1,0:T(8,128)(2,1)} %constant.81.clone.f1l) | copy-start | bytes 1572868
  255.6 9.2 %copy-start.3 = (bf16[512,512]{1,0:T(8,128)(2,1)S(1)}, bf16[512,512]{1,0:T(8,128)(2,1)}, u32[]{:S(2)}) copy-start(bf16[512,512]{1,0:T(8,128)(2,1)} %constant.80.clone.f1h) | copy-start | bytes 1572868
  255.6 9.1 %copy-start.4 = (bf16[256,256]{1,0:T(8,128)(2,1)S(1)}, bf16[256,256]{1,0:T(8,128)(2,1)}, u32[]{:S(2)}) copy-start(bf16[256,256]{1,0:T(8,128)(2,1)} %constant.83.clone.rl.refs_1_) | copy-start | bytes 393220
  255.6 9.1 %copy-start.5 = (bf16[256,256]{1,0:T(8,128)(2,1)S(1)}, bf16[256,256]{1,0:T(8,128)(2,1)}, u32[]{:S(2)}) copy-start(bf16[256,256]{1,0:T(8,128)(2,1)} %constant.82.clone.rh.refs_0_) | copy-start | bytes 393220
  255.6 9.1 %copy-start.16 = (bf16[256,256]{1,0:T(8,128)(2,1)S(1)}, bf16[256,256]{1,0:T(8,128)(2,1)}, u32[]{:S(2)}) copy-start(bf16[256,256]{1,0:T(8,128)(2,1)} %constant.79.clone.f2l) | copy-start | bytes 393220
  255.6 9.1 %copy-start.17 = (bf16[256,256]{1,0:T(8,128)(2,1)S(1)}, bf16[256,256]{1,0:T(8,128)(2,1)}, u32[]{:S(2)}) copy-start(bf16[256,256]{1,0:T(8,128)(2,1)} %constant.78.clone.f2h) | copy-start | bytes 393220
  255.7 9.1 %copy-start.18 = (bf16[256,256]{1,0:T(8,128)(2,1)S(1)}, bf16[256,256]{1,0:T(8,128)(2,1)}, u32[]{:S(2)}) copy-start(bf16[256,256]{1,0:T(8,128)(2,1)} %constant.77.clone.f0l) | copy-start | bytes 393220
  255.7 9.1 %copy-start.19 = (bf16[256,256]{1,0:T(8,128)(2,1)S(1)}, bf16[256,256]{1,0:T(8,128)(2,1)}, u32[]{:S(2)}) copy-start(bf16[256,256]{1,0:T(8,128)(2,1)} %constant.76.clone.f0h) | copy-start | bytes 393220
  271.3 2.0 copy-start.20
  279.7 2.0 copy-start.22
  281.7 25.3 %copy-start = (bf16[512,512]{1,0:T(8,128)(2,1)S(1)}, bf16[512,512]{1,0:T(8,128)(2,1)}, u32[]{:S(2)}) copy-start(bf16[512,512]{1,0:T(8,128)(2,1)} %constant.91.clone.refs_9_) | copy-start | bytes 1572868
  281.7 25.3 %copy-start.1 = (bf16[512,512]{1,0:T(8,128)(2,1)S(1)}, bf16[512,512]{1,0:T(8,128)(2,1)}, u32[]{:S(2)}) copy-start(bf16[512,512]{1,0:T(8,128)(2,1)} %constant.90.clone.refs_8_) | copy-start | bytes 1572868
  281.7 25.3 %copy-start.6 = (bf16[256,256]{1,0:T(8,128)(2,1)S(1)}, bf16[256,256]{1,0:T(8,128)(2,1)}, u32[]{:S(2)}) copy-start(bf16[256,256]{1,0:T(8,128)(2,1)} %constant.95.clone.refs_13_) | copy-start | bytes 393220
  281.7 25.3 %copy-start.7 = (bf16[256,256]{1,0:T(8,128)(2,1)S(1)}, bf16[256,256]{1,0:T(8,128)(2,1)}, u32[]{:S(2)}) copy-start(bf16[256,256]{1,0:T(8,128)(2,1)} %constant.94.clone.refs_12_) | copy-start | bytes 393220
  281.7 25.3 %copy-start.8 = (bf16[256,256]{1,0:T(8,128)(2,1)S(1)}, bf16[256,256]{1,0:T(8,128)(2,1)}, u32[]{:S(2)}) copy-start(bf16[256,256]{1,0:T(8,128)(2,1)} %constant.93.clone.refs_11_) | copy-start | bytes 393220
  281.8 25.3 %copy-start.9 = (bf16[256,256]{1,0:T(8,128)(2,1)S(1)}, bf16[256,256]{1,0:T(8,128)(2,1)}, u32[]{:S(2)}) copy-start(bf16[256,256]{1,0:T(8,128)(2,1)} %constant.92.clone.refs_10_) | copy-start | bytes 393220
  281.8 25.3 %copy-start.10 = (bf16[256,256]{1,0:T(8,128)(2,1)S(1)}, bf16[256,256]{1,0:T(8,128)(2,1)}, u32[]{:S(2)}) copy-start(bf16[256,256]{1,0:T(8,128)(2,1)} %constant.89.clone.refs_7_) | copy-start | bytes 393220
  281.8 25.3 %copy-start.11 = (bf16[256,256]{1,0:T(8,128)(2,1)S(1)}, bf16[256,256]{1,0:T(8,128)(2,1)}, u32[]{:S(2)}) copy-start(bf16[256,256]{1,0:T(8,128)(2,1)} %constant.88.clone.refs_6_) | copy-start | bytes 393220
  281.8 25.3 %copy-start.12 = (bf16[256,256]{1,0:T(8,128)(2,1)S(1)}, bf16[256,256]{1,0:T(8,128)(2,1)}, u32[]{:S(2)}) copy-start(bf16[256,256]{1,0:T(8,128)(2,1)} %constant.87.clone.refs_5_) | copy-start | bytes 393220
  281.8 25.3 %copy-start.13 = (bf16[256,256]{1,0:T(8,128)(2,1)S(1)}, bf16[256,256]{1,0:T(8,128)(2,1)}, u32[]{:S(2)}) copy-start(bf16[256,256]{1,0:T(8,128)(2,1)} %constant.86.clone.refs_4_) | copy-start | bytes 393220
  281.8 25.3 %copy-start.14 = (bf16[256,256]{1,0:T(8,128)(2,1)S(1)}, bf16[256,256]{1,0:T(8,128)(2,1)}, u32[]{:S(2)}) copy-start(bf16[256,256]{1,0:T(8,128)(2,1)} %constant.85.clone.refs_3_) | copy-start | bytes 393220
  281.8 25.3 %copy-start.15 = (bf16[256,256]{1,0:T(8,128)(2,1)S(1)}, bf16[256,256]{1,0:T(8,128)(2,1)}, u32[]{:S(2)}) copy-start(bf16[256,256]{1,0:T(8,128)(2,1)} %constant.84.clone.refs_2_) | copy-start | bytes 393220
  305.1 2.0 copy-start.23
  326.0 2.0 copy-start.21
  340.4 37.2 %collective-permute-start.3 = (f32[128,1024]{1,0:T(8,128)S(1)}, f32[128,1024]{1,0:T(8,128)S(1)}, u32[]{:S(2)}, u32[]{:S(2)}) collective-permute-start(f32[128,1024]{1,0:T(8,128)S(1)} %shard_map.227), channel_id=1, source_target_pairs={{0,0},{4,1},{1,2},{5,3},{2,4},{6,5},{3,6},{7,7},{8,8},{12,9},{9,10... | collective-permute-start | bytes 1572872 | tf_op jit(solution)/shard_map/ppermute | solution.py:361
  342.3 40.9 %collective-permute-start.4 = (f32[128,1024]{1,0:T(8,128)S(1)}, f32[128,1024]{1,0:T(8,128)S(1)}, u32[]{:S(2)}, u32[]{:S(2)}) collective-permute-start(f32[128,1024]{1,0:T(8,128)S(1)} %shard_map.225), channel_id=1, source_target_pairs={{0,0},{4,1},{1,2},{5,3},{2,4},{6,5},{3,6},{7,7},{8,8},{12,9},{9,10... | collective-permute-start | bytes 1572872 | tf_op jit(solution)/shard_map/ppermute | solution.py:361
